TPU v7x, 32 devices: a whole 2x2x4 slice. The times are simulated.
32 devices in a mesh: section: 2 (over core), row: 8 (over z, y), col: 2 (over x).
Axes of the slice: x: 2, y: 2, z: 4, core: 2. Of those that a mesh axis runs over, the one named last changes fastest.
Arguments:
- hidden_in: bfloat16 [8, 256, 3072], P('row', None, 'col')
- patch_ends: int32 [8, 4], P('row'), may hold values from 1 to 256, as said below
- timestep: int32 [8], P('row'), may hold values from 0 to 999
- mod_weight: bfloat16 [2, 256, 3, 3072], P('section'), may hold values from -0.75 to 0.75
- qkv_weight: bfloat16 [2, 3072, 3, 3072], P('section', 'row', None, 'col'), may hold values from -0.109375 to 0.109375
- out_weight: bfloat16 [2, 3072, 3072], P('section', 'col', 'row'), may hold values from -0.109375 to 0.109375
- stale_keys: bfloat16 [2, 8, 256, 3072], P('section', 'row', None, 'col'), may hold values from -1.5 to 1.5
- stale_values: bfloat16 [2, 8, 256, 3072], P('section', 'row', None, 'col'), may hold values from -6 to 6
Outputs:
- layer_out: bfloat16 [2, 8, 256, 3072], P('section', 'row', None, 'col')
Inputs may be any that keep to these rules, and one draw needn't show every extreme that they name: patch_ends rises along each request's 4 patches; each patch holds at least one and at most 64 positions, and in every draw some request has all 4 patches of exactly 64 positions.
All inputs are finite; a program needn't handle non-finite values.
Results may differ from a plain program's by a relative error of at most 0.018.
Values may be sent and summed in bfloat16 or wider, within the bound.
No kernel may reach another device: no remote copies, remote signals or barrier semaphores. Data moves between devices by JAX's collectives and lax.ppermute only.
A program may use at most 128 MiB of HBM per device.

v0:
```python
import math

import jax
import jax.numpy as jnp
from jax import lax
from jax.sharding import PartitionSpec as P

HD = 128
FREQ = 256
NP = 4
PATCH = 64


def passed_along(array, axis, by):
    length = lax.axis_size(axis)
    pairs = [(i, i + by) for i in range(length) if 0 <= i + by < length]
    return lax.ppermute(array, axis, pairs)


def embed_time(timestep, feat_width):
    half_width = feat_width // 2
    frequency = jnp.exp(
        jnp.arange(half_width, dtype=jnp.float32) * (-math.log(10000.0) / half_width)
    )
    angles = timestep.astype(jnp.float32)[:, None] * frequency[None, :]
    return jnp.concatenate([jnp.cos(angles), jnp.sin(angles)], axis=1).astype(jnp.bfloat16)


def head_norm(raw_proj):
    shaped = raw_proj.reshape(raw_proj.shape[:-1] + (raw_proj.shape[-1] // HD, HD))
    scaled = shaped / jnp.sqrt(jnp.mean(shaped * shaped, axis=-1, keepdims=True) + 1e-06)
    return scaled.reshape(raw_proj.shape).astype(jnp.bfloat16)


def slice_one(source, first_row):
    return lax.dynamic_slice_in_dim(source, first_row, PATCH, 0)


def update_one(source, new_rows, first_row):
    return lax.dynamic_update_slice_in_dim(source, new_rows, first_row, 0)


def take_rows(source, row_begin):
    return jax.vmap(slice_one)(source, row_begin)


def put_rows(source, new_rows, row_begin, row_count, is_active):
    previous = take_rows(source, row_begin)
    keep_new = (jnp.arange(PATCH)[None, :, None] < row_count[:, None, None]) & is_active
    merged = jnp.where(keep_new, new_rows, previous)
    return jax.vmap(update_one)(source, merged, row_begin)


def attend_rows(queries, key_rows, value_rows, key_ok):
    requests = queries.shape[0]
    query_heads = queries.reshape(requests, queries.shape[1], -1, HD)
    key_heads = key_rows.reshape(requests, key_rows.shape[1], -1, HD)
    value_heads = value_rows.reshape(requests, value_rows.shape[1], -1, HD)
    scores = jnp.einsum(
        "bqhd,bkhd->bhqk", query_heads, key_heads, preferred_element_type=jnp.float32
    ) / math.sqrt(HD)
    weights = jnp.exp(scores) * key_ok[:, None, None, :]
    weights = (weights / jnp.sum(weights, axis=-1, keepdims=True)).astype(jnp.bfloat16)
    mixed = jnp.einsum("bhqk,bkhd->bqhd", weights, value_heads, preferred_element_type=jnp.float32)
    return mixed.reshape(queries.shape).astype(jnp.bfloat16)


def modulated_rows(patch_rows, shift_vec, scale_vec, col_index, col_width):
    feat_width = shift_vec.shape[-1]
    as_float = patch_rows.astype(jnp.float32)
    sum_rows, sum_squares = lax.psum(
        (jnp.sum(as_float, axis=-1), jnp.sum(as_float * as_float, axis=-1)), "col"
    )
    row_mean = (sum_rows / feat_width)[:, :, None]
    row_var = (sum_squares / feat_width)[:, :, None] - row_mean * row_mean
    shift_own = lax.dynamic_slice_in_dim(shift_vec, col_index * col_width, col_width, 1)
    scale_own = lax.dynamic_slice_in_dim(scale_vec, col_index * col_width, col_width, 1)
    normed = (as_float - row_mean) / jnp.sqrt(row_var + 1e-06)
    local_rows = (normed * (1.0 + scale_own[:, None, :]) + shift_own[:, None, :]).astype(
        jnp.bfloat16
    )
    return lax.all_gather(local_rows, "col", axis=2, tiled=True)


def shards(
    hidden_in, patch_ends, timestep, mod_weight, qkv_weight, out_weight, stale_keys, stale_values
):
    section_index = lax.axis_index("section")
    col_index = lax.axis_index("col")
    requests, slot_len, col_width = hidden_in.shape
    feat_width = mod_weight.shape[-1]
    qkv_full = lax.all_gather(qkv_weight, "row", axis=1, tiled=True)
    out_full = lax.all_gather(out_weight, "row", axis=2, tiled=True)
    qkv_matrix = qkv_full[0].reshape(feat_width, 3 * col_width)
    out_matrix = out_full[0]
    time_feats = embed_time(timestep, FREQ)
    modulation = jnp.dot(
        time_feats, mod_weight[0].reshape(FREQ, 3 * feat_width), preferred_element_type=jnp.float32
    ).reshape(requests, 3, feat_width)
    shift_vec = modulation[:, 0]
    scale_vec = modulation[:, 1]
    gate_own = lax.dynamic_slice_in_dim(modulation[:, 2], col_index * col_width, col_width, 1)
    padding = jnp.zeros((requests, PATCH, col_width), jnp.bfloat16)
    input_pad = jnp.concatenate([hidden_in, padding], axis=1)
    key_cache = jnp.concatenate([stale_keys[0], padding], axis=1)
    value_cache = jnp.concatenate([stale_values[0], padding], axis=1)
    result_pad = jnp.zeros((requests, slot_len + PATCH, col_width), jnp.bfloat16)
    patch_starts = jnp.concatenate(
        [jnp.zeros((requests, 1), jnp.int32), patch_ends[:, : NP - 1]], axis=1
    )
    seq_len = patch_ends[:, NP - 1]
    key_ok = (jnp.arange(slot_len)[None, :] < seq_len[:, None]).astype(jnp.float32)
    row_ids = jnp.arange(PATCH)
    received = padding
    for step_index in range(NP + 1):
        offset = step_index - section_index
        is_active = (offset >= 0) & (offset < NP)
        patch_index = jnp.clip(offset, 0, NP - 1)
        row_begin = jnp.take(patch_starts, patch_index, axis=1)
        row_count = jnp.take(patch_ends, patch_index, axis=1) - row_begin
        patch_rows = jnp.where(section_index == 0, take_rows(input_pad, row_begin), received)
        modulated = modulated_rows(patch_rows, shift_vec, scale_vec, col_index, col_width)
        projected = jnp.dot(
            modulated.reshape(-1, feat_width), qkv_matrix, preferred_element_type=jnp.float32
        ).reshape(requests, PATCH, 3, col_width)
        queries = head_norm(projected[:, :, 0])
        key_cache = put_rows(
            key_cache, head_norm(projected[:, :, 1]), row_begin, row_count, is_active
        )
        value_cache = put_rows(
            value_cache, projected[:, :, 2].astype(jnp.bfloat16), row_begin, row_count, is_active
        )
        attended = attend_rows(queries, key_cache[:, :slot_len], value_cache[:, :slot_len], key_ok)
        partial_out = jnp.dot(
            attended.reshape(-1, col_width), out_matrix, preferred_element_type=jnp.float32
        ).reshape(requests, PATCH, feat_width)
        summed = lax.psum_scatter(
            partial_out.astype(jnp.bfloat16), "col", scatter_dimension=2, tiled=True
        ).astype(jnp.float32)
        updated = patch_rows.astype(jnp.float32) + gate_own[:, None, :] * summed
        within = row_ids[None, :, None] < row_count[:, None, None]
        new_rows = jnp.where(within, updated, 0.0).astype(jnp.bfloat16)
        result_pad = put_rows(result_pad, new_rows, row_begin, row_count, is_active)
        if step_index < NP:
            received = passed_along(new_rows, "section", 1)
    return result_pad[None, :, :slot_len]


def solution(mesh):
    return jax.shard_map(
        shards,
        mesh=mesh,
        in_specs=(
            P("row", None, "col"),
            P("row", None),
            P("row"),
            P("section", None, None, None),
            P("section", "row", None, "col"),
            P("section", "col", "row"),
            P("section", "row", None, "col"),
            P("section", "row", None, "col"),
        ),
        out_specs=P("section", "row", None, "col"),
        check_vma=False,
    )
```

profile of v0, /device:TPU:0, one launch (start us, length us, event | category | flops | bytes accessed | tf_op | source)
XLA Modules:
  0.0 1037.5 jit_solution(9447282435841489065)
XLA Ops:
  6.5 6.1 copy.30
  18.2 6.7 copy.29
  26.0 6.4 all-reduce.7
  32.4 3.6 fusion.20
  38.2 6.9 all_gather.21
  50.7 5.2 and_reduce_fusion
  55.8 499.2 %all-gather.3.cloned.1.call-done = bf16[1,3072,3,1536]{1,3,2,0:T(8,128)(2,1)} async-done(((bf16[1,384,3,1536]{1,3,2,0:T(8,128)(2,1)}), bf16[1,3072,3,1536]{1,3,2,0:T(8,128)(2,1)}) %all-gather.3.cloned.1.call-update) | async-done | bytes 28311568 | tf_op jit(solution)/shard_map/all_gather | solution.py:92
  555.1 14.7 %fusion.52 = f32[1,64,3,1536]{3,1,2,0:T(8,128)} fusion(bf16[1,3072,3,1536]{1,3,2,0:T(8,128)(2,1)} %all-gather.3.cloned.1.call-done, bf16[1,64,3072]{2,1,0:T(8,128)(2,1)} %all_gather.21), kind=kOutput, calls=%fused_computation.32 | convolution fusion | flops 1811939328 | bytes 29884416 | tf_op jit(solution)/shard_map/dot_general | solution.py:123
  584.8 3.7 fusion.138
  604.7 90.6 %all-gather.5.cloned.1.call-done = bf16[1,1536,3072]{2,1,0:T(8,128)(2,1)} async-done(((bf16[1,1536,384]{2,1,0:T(8,128)(2,1)}), bf16[1,1536,3072]{2,1,0:T(8,128)(2,1)}) %all-gather.5.cloned.1.call-update) | async-done | bytes 9437200 | tf_op jit(solution)/shard_map/all_gather | solution.py:93
  695.3 6.2 fusion.49
  703.5 9.5 reduce-scatter.6.cloned.1.call-done
  720.8 4.9 all-reduce.6
  725.9 6.9 all_gather.24
  732.8 14.9 %fusion.55 = f32[1,64,3,1536]{3,1,2,0:T(8,128)} fusion(bf16[1,3072,3,1536]{1,3,2,0:T(8,128)(2,1)} %all-gather.3.cloned.1.call-done, bf16[1,64,3072]{2,1,0:T(8,128)(2,1)S(1)} %all_gather.24), kind=kOutput, calls=%fused_computation.33 | convolution fusion | flops 1811939328 | bytes 29884416 | tf_op jit(solution)/shard_map/dot_general | solution.py:123
  774.9 6.2 fusion.46
  784.6 9.7 reduce-scatter.8.cloned.1.call-done
  800.7 5.0 all-reduce.5
  805.8 6.9 all_gather.25
  812.7 14.9 %fusion.58 = f32[1,64,3,1536]{3,1,2,0:T(8,128)} fusion(bf16[1,3072,3,1536]{1,3,2,0:T(8,128)(2,1)} %all-gather.3.cloned.1.call-done, bf16[1,64,3072]{2,1,0:T(8,128)(2,1)S(1)} %all_gather.25), kind=kOutput, calls=%fused_computation.34 | convolution fusion | flops 1811939328 | bytes 29884416 | tf_op jit(solution)/shard_map/dot_general | solution.py:123
  855.0 6.2 fusion.43
  863.8 10.7 %reduce-scatter.10.cloned.1.call-done = bf16[1,64,1536]{2,1,0:T(8,128)(2,1)} async-done(((bf16[1,64,3072]{2,1,0:T(8,128)(2,1)}), bf16[1,64,1536]{2,1,0:T(8,128)(2,1)}) %reduce-scatter.10.cloned.1.call-update) | async-done | bytes 196624 | tf_op jit(solution)/shard_map/reduce_scatter | solution.py:137
  881.0 5.0 all-reduce.4
  886.1 6.9 all_gather.26
  893.0 14.9 %fusion.61 = f32[1,64,3,1536]{3,1,2,0:T(8,128)} fusion(bf16[1,3072,3,1536]{1,3,2,0:T(8,128)(2,1)} %all-gather.3.cloned.1.call-done, bf16[1,64,3072]{2,1,0:T(8,128)(2,1)S(1)} %all_gather.26), kind=kOutput, calls=%fused_computation.35 | convolution fusion | flops 1811939328 | bytes 29884416 | tf_op jit(solution)/shard_map/dot_general | solution.py:123
  935.1 6.2 fusion.40
  943.9 10.7 %reduce-scatter.12.cloned.1.call-done = bf16[1,64,1536]{2,1,0:T(8,128)(2,1)} async-done(((bf16[1,64,3072]{2,1,0:T(8,128)(2,1)}), bf16[1,64,1536]{2,1,0:T(8,128)(2,1)}) %reduce-scatter.12.cloned.1.call-update) | async-done | bytes 196624 | tf_op jit(solution)/shard_map/reduce_scatter | solution.py:137
  960.9 5.0 all-reduce.3
  966.1 6.9 all_gather.27
  973.0 14.9 %fusion.64 = f32[1,64,3,1536]{3,1,2,0:T(8,128)} fusion(bf16[1,3072,3,1536]{1,3,2,0:T(8,128)(2,1)} %all-gather.3.cloned.1.call-done, bf16[1,64,3072]{2,1,0:T(8,128)(2,1)S(1)} %all_gather.27), kind=kOutput, calls=%fused_computation.36 | convolution fusion | flops 1811939328 | bytes 29884416 | tf_op jit(solution)/shard_map/dot_general | solution.py:123
  1005.3 6.3 fusion.37
  1013.7 11.2 %reduce-scatter.14.cloned.1.call-done = bf16[1,64,1536]{2,1,0:T(8,128)(2,1)} async-done(((bf16[1,64,3072]{2,1,0:T(8,128)(2,1)}), bf16[1,64,1536]{2,1,0:T(8,128)(2,1)}) %reduce-scatter.14.cloned.1.call-update) | async-done | bytes 196624 | tf_op jit(solution)/shard_map/reduce_scatter | solution.py:137
  (262 shorter events, 182.7 us)
Async XLA Ops:
  6.5 548.5 %all-gather.3.cloned.1.call-start = ((), (), s32[]{:S(2)}) async-start(), calls=%async_computation.5 | async-start | bytes 31850496 | tf_op jit(solution)/shard_map/all_gather | solution.py:92
  12.7 682.6 %all-gather.5.cloned.1.call-start = ((), (), s32[]{:S(2)}) async-start(), calls=%async_computation.6 | async-start | bytes 10616832 | tf_op jit(solution)/shard_map/all_gather | solution.py:93
  13.5 699.5 %reduce-scatter.6.cloned.1.call-start = ((), (), s32[]{:S(2)}) async-start(), calls=%async_computation.7 | async-start | bytes 589824 | tf_op jit(solution)/shard_map/reduce_scatter | solution.py:137
  36.7 533.0 %copy-start.16 = (f32[1536]{0:T(1024)}, f32[1536]{0:T(1024)S(1)}, u32[]{:S(2)}) copy-start(f32[1536]{0:T(1024)S(1)} %fusion.191) | copy-start | bytes 18436
  571.9 29.4 %copy-start.22 = (f32[256]{0:T(256)S(1)}, f32[256]{0:T(256)}, u32[]{:S(2)}) copy-start(f32[256]{0:T(256)} %compare_convert_fusion) | copy-start | bytes 3076
  604.5 97.6 %copy-start.21 = (f32[1,1,3072]{2,0,1:T(1,128)S(1)}, f32[1,1,3072]{2,0,1:T(1,128)}, u32[]{:S(2)}) copy-start(f32[1,1,3072]{2,0,1:T(1,128)} %get-tuple-element.589) | copy-start | bytes 36868
  604.5 97.7 %copy-start.26 = (s32[1,2]{1,0:T(1,128)S(1)}, s32[1,2]{1,0:T(1,128)}, u32[]{:S(2)}) copy-start(s32[1,2]{1,0:T(1,128)} %get-tuple-element.606) | copy-start | bytes 28
  604.5 98.3 %copy-start.25 = (s32[1,2]{1,0:T(1,128)S(1)}, s32[1,2]{1,0:T(1,128)}, u32[]{:S(2)}) copy-start(s32[1,2]{1,0:T(1,128)} %get-tuple-element.605) | copy-start | bytes 28
  604.5 108.5 %copy-start.27 = (pred[64]{0:T(512)(128)(4,1)S(1)}, pred[64]{0:T(512)(128)(4,1)}, u32[]{:S(2)}) copy-start(pred[64]{0:T(512)(128)(4,1)} %broadcast_and_fusion.4) | copy-start | bytes 196
  604.6 112.6 %copy-start.36 = (s32[3]{0:T(128)S(1)}, s32[3]{0:T(128)}, u32[]{:S(2)}) copy-start(s32[3]{0:T(128)} %constant.478.clone.1) | copy-start | bytes 40
  695.3 30.4 %copy-start.17 = (f32[1536]{0:T(1024)S(1)}, f32[1536]{0:T(1024)}, u32[]{:S(2)}) copy-start(f32[1536]{0:T(1024)} %copy-done.16) | copy-start | bytes 18436
  701.5 92.8 %reduce-scatter.8.cloned.1.call-start = ((), (), s32[]{:S(2)}) async-start(), calls=%async_computation.8 | async-start | bytes 589824 | tf_op jit(solution)/shard_map/reduce_scatter | solution.py:137
  715.4 5.2 collective-permute-start
  717.1 38.8 %copy-start.30 = (pred[64]{0:T(512)(128)(4,1)}, pred[64]{0:T(512)(128)(4,1)S(1)}, u32[]{:S(2)}) copy-start(pred[64]{0:T(512)(128)(4,1)S(1)} %broadcast_and_fusion.3) | copy-start | bytes 196
  720.8 26.9 %copy-start.6 = (bf16[1,64,1536]{2,1,0:T(8,128)(2,1)}, bf16[1,64,1536]{2,1,0:T(8,128)(2,1)S(1)}, u32[]{:S(2)}) copy-start(bf16[1,64,1536]{2,1,0:T(8,128)(2,1)S(1)} %get-tuple-element.561) | copy-start | bytes 589828
  774.8 30.8 %copy-start.18 = (f32[1536]{0:T(1024)S(1)}, f32[1536]{0:T(1024)}, u32[]{:S(2)}) copy-start(f32[1536]{0:T(1024)} %copy-done.16) | copy-start | bytes 18436
  781.1 93.4 %reduce-scatter.10.cloned.1.call-start = ((), (), s32[]{:S(2)}) async-start(), calls=%async_computation.9 | async-start | bytes 589824 | tf_op jit(solution)/shard_map/reduce_scatter | solution.py:137
  797.7 2.8 collective-permute-start.1
  800.0 35.9 %copy-start.32 = (pred[64]{0:T(512)(128)(4,1)}, pred[64]{0:T(512)(128)(4,1)S(1)}, u32[]{:S(2)}) copy-start(pred[64]{0:T(512)(128)(4,1)S(1)} %broadcast_and_fusion.2) | copy-start | bytes 196
  800.7 26.9 %copy-start.8 = (bf16[1,64,1536]{2,1,0:T(8,128)(2,1)}, bf16[1,64,1536]{2,1,0:T(8,128)(2,1)S(1)}, u32[]{:S(2)}) copy-start(bf16[1,64,1536]{2,1,0:T(8,128)(2,1)S(1)} %get-tuple-element.558) | copy-start | bytes 589828
  855.0 30.9 %copy-start.19 = (f32[1536]{0:T(1024)S(1)}, f32[1536]{0:T(1024)}, u32[]{:S(2)}) copy-start(f32[1536]{0:T(1024)} %copy-done.16) | copy-start | bytes 18436
  861.3 93.3 %reduce-scatter.12.cloned.1.call-start = ((), (), s32[]{:S(2)}) async-start(), calls=%async_computation.10 | async-start | bytes 589824 | tf_op jit(solution)/shard_map/reduce_scatter | solution.py:137
  877.9 2.8 collective-permute-start.2
  880.3 35.9 %copy-start.34 = (pred[64]{0:T(512)(128)(4,1)}, pred[64]{0:T(512)(128)(4,1)S(1)}, u32[]{:S(2)}) copy-start(pred[64]{0:T(512)(128)(4,1)S(1)} %broadcast_and_fusion.1) | copy-start | bytes 196
  881.0 26.9 %copy-start.10 = (bf16[1,64,1536]{2,1,0:T(8,128)(2,1)}, bf16[1,64,1536]{2,1,0:T(8,128)(2,1)S(1)}, u32[]{:S(2)}) copy-start(bf16[1,64,1536]{2,1,0:T(8,128)(2,1)S(1)} %get-tuple-element.555) | copy-start | bytes 589828
  935.1 30.8 %copy-start.20 = (f32[1536]{0:T(1024)S(1)}, f32[1536]{0:T(1024)}, u32[]{:S(2)}) copy-start(f32[1536]{0:T(1024)} %copy-done.16) | copy-start | bytes 18436
  941.3 83.5 %reduce-scatter.14.cloned.1.call-start = ((), (), s32[]{:S(2)}) async-start(), calls=%async_computation.11 | async-start | bytes 589824 | tf_op jit(solution)/shard_map/reduce_scatter | solution.py:137
  957.9 2.8 collective-permute-start.3
  960.4 34.0 %copy-start.28 = (pred[64]{0:T(512)(128)(4,1)}, pred[64]{0:T(512)(128)(4,1)S(1)}, u32[]{:S(2)}) copy-start(pred[64]{0:T(512)(128)(4,1)S(1)} %broadcast_and_fusion) | copy-start | bytes 196
  960.9 27.0 %copy-start.4 = (bf16[1,64,1536]{2,1,0:T(8,128)(2,1)}, bf16[1,64,1536]{2,1,0:T(8,128)(2,1)S(1)}, u32[]{:S(2)}) copy-start(bf16[1,64,1536]{2,1,0:T(8,128)(2,1)S(1)} %get-tuple-element.552) | copy-start | bytes 589828
  1005.1 19.7 %copy-start.5 = (bf16[1,64,1536]{2,1,0:T(8,128)(2,1)S(1)}, bf16[1,64,1536]{2,1,0:T(8,128)(2,1)}, u32[]{:S(2)}) copy-start(bf16[1,64,1536]{2,1,0:T(8,128)(2,1)} %copy-done.4) | copy-start | bytes 589828
  1005.2 19.7 %copy-start.29 = (pred[64]{0:T(512)(128)(4,1)S(1)}, pred[64]{0:T(512)(128)(4,1)}, u32[]{:S(2)}) copy-start(pred[64]{0:T(512)(128)(4,1)} %copy-done.28) | copy-start | bytes 196
  (16 other events, 220.0 us)
Sparse Core Ops, SparseCore 0:
  12.8 542.1 all-gather.2
  557.1 138.1 all-gather.4
  701.7 11.2 reduce-scatter.5
  781.2 13.1 reduce-scatter.7
  861.4 13.0 reduce-scatter.9
  941.5 13.1 reduce-scatter.11
  1011.7 13.1 reduce-scatter.13
where the time goes:
time: 1050 us; the launch traced here: 1040 us
  waiting for transfers between devices  644 us (61%)
  matrix products  124 us (12%)
  local copies, waits for them, and re-layouts  105 us (10%)
  other arithmetic  74.7 us (7%)
  blocking collectives  60.7 us (6%)
  between operations  21.7 us (2%)
    all_gather x1, waiting for transfers between devices, shards(): qkv_full = lax.all_gather(qkv_weight, 'row', axis=1, tiled=True)  499 us
    all_gather x1, waiting for transfers between devices, shards(): out_full = lax.all_gather(out_weight, 'row', axis=2, tiled=True)  90.6 us
    dot_general x5, matrix products, shards(): jnp.dot(modulated.reshape(-1, feat_width), qkv_matrix, preferred_element_...  74.2 us
    reduce_scatter x5, waiting for transfers between devices, shards(): lax.psum_scatter(partial_out.astype(jnp.bfloat16), 'col', scatter_dimensi...  51.9 us
    another operation x13, other arithmetic  40.9 us
    scatter x15, local copies, waits for them, and re-layouts, update_one(): return lax.dynamic_update_slice_in_dim(source, new_rows, first_row, 0)  35.2 us
    all_gather x5, blocking collectives, modulated_rows(): return lax.all_gather(local_rows, 'col', axis=2, tiled=True)  34.5 us
    dot_general x5, matrix products, shards(): jnp.dot(attended.reshape(-1, col_width), out_matrix, preferred_element_ty...  31.1 us
  transfers between devices with their start and end apart: 11, of which 10 were waited for; matrix products, arithmetic and copies ran while one was open for 9% of the time, Pallas kernels for 0%

commit v1 on v0

v1 whole, which is shorter than its diff:
```python
import functools
import math

import jax
import jax.numpy as jnp
from jax import lax
from jax.experimental import pallas as pl
from jax.experimental.pallas import tpu as pltpu
from jax.sharding import PartitionSpec as P

HD = 128
FREQ = 256
NP = 4
AXES = ("section", "row", "col")
VMEM_LIMIT = 56 * 1024 * 1024


def send_to(array, where):
    ns, nr, nc = (lax.axis_size(axis) for axis in AXES)
    pairs = []
    for s in range(ns):
        for i in range(nr):
            for c in range(nc):
                ts, ti, tc = where(s, i, c)
                pairs.append(((s * nr + i) * nc + c, (ts * nr + ti) * nc + tc))
    return lax.ppermute(array, AXES, pairs)


def to_core(array):
    return send_to(array, lambda s, i, c: (1 - s, i, c))


def to_row(array, bit):
    return send_to(array, lambda s, i, c: (s, i ^ bit, c))


def after(array, *others):
    return lax.optimization_barrier((array,) + others)[0]


def pick(array, index):
    return lax.dynamic_index_in_dim(array, index, 0, keepdims=False)


def embed_time(timestep):
    half_width = FREQ // 2
    frequency = jnp.exp(
        jnp.arange(half_width, dtype=jnp.float32) * (-math.log(10000.0) / half_width)
    )
    angles = timestep.astype(jnp.float32)[:, None] * frequency[None, :]
    return jnp.concatenate([jnp.cos(angles), jnp.sin(angles)], axis=1).astype(jnp.bfloat16)


def any_spec():
    return pl.BlockSpec(memory_space=pl.ANY)


def vmem_spec():
    return pl.BlockSpec(memory_space=pltpu.VMEM)


def attend_kernel(plan, ends_ref, mod_ref, *refs):
    slots, slot_len, cols, n_x, n_w, kr, bw, wc = plan
    x_refs, refs = refs[:n_x], refs[n_x:]
    w_refs, refs = refs[:n_w], refs[n_w:]
    kv_refs, refs = refs[:slots], refs[slots:]
    out_ref, xv, xm, wv, kvv, x_sem, w_sem, kv_sem = refs
    s, i, c = (lax.axis_index(axis) for axis in AXES)
    half = slot_len // 2
    x_copies, w_copies, kv_copies = [], [], []
    place = 0
    for slot in range(slots):
        for dc in range(cols):
            for h in range(2):
                col = lax.rem(c + cols - dc, cols)
                row = slot * slot_len + jnp.where(s == h, 0, half)
                row = pl.multiple_of(row, half)
                x_copies.append(
                    pltpu.make_async_copy(
                        x_refs[place], xv.at[col, pl.ds(row, half), :], x_sem.at[place]
                    )
                )
                place += 1
    for d in range(n_w):
        rows = pl.ds(pl.multiple_of((i ^ d) * kr, 32), kr)
        w_copies.append(pltpu.make_async_copy(w_refs[d], wv.at[:, rows, :], w_sem.at[d]))
    for slot in range(slots):
        kv_copies.append(pltpu.make_async_copy(kv_refs[slot], kvv.at[slot], kv_sem.at[slot]))
    for copy in x_copies + w_copies + kv_copies:
        copy.start()
    for copy in x_copies:
        copy.wait()
    feat = cols * wc
    for slot in range(slots):
        rows = pl.ds(slot * slot_len, slot_len)
        total = jnp.zeros((slot_len, 1), jnp.float32)
        squares = jnp.zeros((slot_len, 1), jnp.float32)
        for col in range(cols):
            part = xv[col, rows, :].astype(jnp.float32)
            total += jnp.sum(part, axis=-1, keepdims=True)
            squares += jnp.sum(part * part, axis=-1, keepdims=True)
        mean = total / feat
        var = squares / feat - mean * mean
        inverse = 1.0 / jnp.sqrt(var + 1e-06)
        for col in range(cols):
            span = pl.ds(col * wc, wc)
            part = xv[col, rows, :].astype(jnp.float32)
            shift = mod_ref[slot, 0:1, span]
            scale = mod_ref[slot, 1:2, span]
            xm[rows, span] = ((part - mean) * inverse * (1.0 + scale) + shift).astype(jnp.bfloat16)
    for copy in w_copies + kv_copies:
        copy.wait()
    key_at = lax.broadcasted_iota(jnp.int32, (slot_len, slot_len), 1)
    query_at = lax.broadcasted_iota(jnp.int32, (slot_len, slot_len), 0)
    contract = (((1,), (1,)), ((), ()))
    for slot in range(slots):
        rows = pl.ds(slot * slot_len, slot_len)
        raw = [
            jnp.dot(xm[rows, :], wv[t], preferred_element_type=jnp.float32) for t in range(3)
        ]
        limit = jnp.full((slot_len, slot_len), ends_ref[slot, NP - 1], jnp.int32)
        for m in range(NP - 2, -1, -1):
            limit = jnp.where(query_at < ends_ref[slot, m], ends_ref[slot, m], limit)
        fresh = key_at < limit
        valid = key_at < ends_ref[slot, NP - 1]
        for head in range(bw // HD):
            lanes = slice(head * HD, (head + 1) * HD)

            def normed(block):
                return (
                    block / jnp.sqrt(jnp.mean(block * block, axis=-1, keepdims=True) + 1e-06)
                ).astype(jnp.bfloat16)

            query = normed(raw[0][:, lanes])
            key = normed(raw[1][:, lanes])
            value = raw[2][:, lanes].astype(jnp.bfloat16)
            old_key = kvv[slot, 0, :, lanes]
            old_value = kvv[slot, 1, :, lanes]
            new_scores = lax.dot_general(query, key, contract, preferred_element_type=jnp.float32)
            old_scores = lax.dot_general(
                query, old_key, contract, preferred_element_type=jnp.float32
            )
            scores = jnp.where(fresh, new_scores, old_scores) * (1.0 / math.sqrt(HD))
            weights = jnp.where(valid, jnp.exp(scores), 0.0)
            weights = weights / jnp.sum(weights, axis=-1, keepdims=True)
            mixed = jnp.dot(
                jnp.where(fresh, weights, 0.0).astype(jnp.bfloat16),
                value,
                preferred_element_type=jnp.float32,
            ) + jnp.dot(
                jnp.where(fresh, 0.0, weights).astype(jnp.bfloat16),
                old_value,
                preferred_element_type=jnp.float32,
            )
            out_ref[rows, lanes] = mixed.astype(jnp.bfloat16)


def out_kernel(plan, attended_ref, *refs):
    slots, slot_len, cols, n_w, nr, bw, wc = plan
    o_refs, refs = refs[:n_w], refs[n_w:]
    keep_ref, pass_ref, ov, o_sem = refs
    s, i, c = (lax.axis_index(axis) for axis in AXES)
    feat = cols * wc
    half = slot_len // 2
    copies = []
    for d in range(n_w):
        start = lax.rem((i ^ d) * nr + feat - c * wc, feat)
        rows = pl.ds(pl.multiple_of(start, 32), nr)
        copies.append(pltpu.make_async_copy(o_refs[d], ov.at[rows, :], o_sem.at[d]))
    for copy in copies:
        copy.start()
    for copy in copies:
        copy.wait()
    contract = (((1,), (1,)), ((), ()))
    blocks = []
    for side in (s, 1 - s):
        for slot in range(slots):
            row = pl.multiple_of(slot * slot_len + side * half, half)
            blocks.append(attended_ref[pl.ds(row, half), :])
    lhs = jnp.concatenate(blocks, axis=0)
    tile = wc // 3
    for first in range(0, feat, tile):
        part = lax.dot_general(
            lhs, ov[first : first + tile, :], contract, preferred_element_type=jnp.float32
        ).astype(jnp.bfloat16)
        part = part.reshape(2, slots, half, tile)
        keep_ref[:, :, first : first + tile] = part[0]
        pass_ref[:, :, first : first + tile] = part[1]


def shards(
    hidden_in, patch_ends, timestep, mod_weight, qkv_weight, out_weight, stale_keys, stale_values
):
    s, i, c = (lax.axis_index(axis) for axis in AXES)
    sections, rows, cols = (lax.axis_size(axis) for axis in AXES)
    _, slot_len, wc = hidden_in.shape
    feat = mod_weight.shape[-1]
    kr = qkv_weight.shape[1]
    nr = out_weight.shape[2]
    half = slot_len // 2
    slots = 2 if (wc // HD) % (2 * sections) == 0 else 1
    bw = wc // (sections * slots)
    row_bits = [1 << b for b in range(rows.bit_length() - 1)]
    split_bit = 2 if slots == 2 else 0
    group_bits = [b for b in reversed(row_bits) if b != split_bit]
    mine_at = (i // 2) % 2 if slots == 2 else 0
    offsets = [0, split_bit] if slots == 2 else [0]

    qkv_blocks = jnp.transpose(
        qkv_weight[0].transpose(1, 0, 2).reshape(3, kr, sections, slots, bw), (2, 3, 0, 1, 4)
    )
    out_blocks = out_weight[0].reshape(sections, slots, bw, nr).transpose(0, 1, 3, 2)
    stale = jnp.stack([stale_keys[0, 0], stale_values[0, 0]])
    stale_blocks = stale.reshape(2, slot_len, sections, slots, bw).transpose(2, 3, 0, 1, 4)

    def both_layers(blocks):
        own, other = pick(blocks, s), to_core(pick(blocks, 1 - s))
        return jnp.where(s == 0, own, other), jnp.where(s == 0, other, own)

    qkv_layers = both_layers(qkv_blocks)
    out_layers = both_layers(out_blocks)
    stale_layers = both_layers(stale_blocks)

    modulation = jnp.einsum(
        "f,kfd->kd",
        embed_time(timestep)[0],
        mod_weight[0].transpose(1, 0, 2),
        preferred_element_type=jnp.float32,
    )
    other_modulation = to_core(modulation)
    mod_layers = (
        jnp.where(s == 0, modulation, other_modulation),
        jnp.where(s == 0, other_modulation, modulation),
    )
    ends = patch_ends[0]
    if slots == 2:
        ends_all = jnp.stack([ends, to_row(ends, split_bit)])
        mod_both = jnp.stack([mod_layers[0][:2], mod_layers[1][:2]])
        mod_other = to_row(mod_both, split_bit)
        mod_slots = [jnp.stack([mod_both[l], mod_other[l]]) for l in range(2)]
    else:
        ends_all = ends[None]
        mod_slots = [mod_layers[l][:2][None] for l in range(2)]

    def spread(own, gate):
        pieces = {0: pick(own, mine_at)}
        if slots == 2:
            sent = pick(own, 1 - mine_at)
            pieces[split_bit] = to_row(after(sent, *gate) if gate else sent, split_bit)
        crossed = []
        for bit in group_bits:
            new = {}
            for d, piece in pieces.items():
                if bit == group_bits[0] and gate:
                    piece = after(piece, *gate)
                new[d ^ bit] = to_row(piece, bit)
            if bit == group_bits[0]:
                crossed = list(new.values())
            pieces.update(new)
        return [pieces[d] for d in range(rows)], crossed

    qkv0, gate_q = spread(qkv_layers[0], ())
    out0, gate_o = spread(out_layers[0], ())
    gate = gate_q + gate_o
    qkv1, gate_q = spread(qkv_layers[1], gate)
    out1, _ = spread(out_layers[1], gate)
    weights = ((qkv0, out0), (qkv1, out1))

    stale_slots = []
    for layer in range(2):
        own = stale_layers[layer]
        block = [pick(own, mine_at)]
        if slots == 2:
            block.append(to_row(pick(own, 1 - mine_at), split_bit))
        stale_slots.append(block)

    places = [(di, dc) for di in offsets for dc in range(cols)]

    def send_place(array, di, dc):
        return send_to(array, lambda si, ii, ci: (si, ii ^ di, (ci + dc) % cols))

    def gather(own_half):
        pieces = []
        for di, dc in places:
            got = own_half if (di, dc) == (0, 0) else send_place(own_half, di, dc)
            pieces.extend([got, to_core(got)])
        return pieces

    def layer_step(layer, x_pieces, x_half):
        qkv_pieces, out_pieces = weights[layer]
        n_w = rows
        plan = (slots, slot_len, cols, len(x_pieces), n_w, kr, bw, wc)
        attended = pl.pallas_call(
            functools.partial(attend_kernel, plan),
            out_shape=jax.ShapeDtypeStruct((slots * slot_len, bw), jnp.bfloat16),
            in_specs=[pl.BlockSpec(memory_space=pltpu.SMEM), vmem_spec()]
            + [any_spec()] * (len(x_pieces) + n_w + slots),
            out_specs=vmem_spec(),
            scratch_shapes=[
                pltpu.VMEM((cols, slots * slot_len, wc), jnp.bfloat16),
                pltpu.VMEM((slots * slot_len, feat), jnp.bfloat16),
                pltpu.VMEM((3, feat, bw), jnp.bfloat16),
                pltpu.VMEM((slots, 2, slot_len, bw), jnp.bfloat16),
                pltpu.SemaphoreType.DMA((len(x_pieces),)),
                pltpu.SemaphoreType.DMA((n_w,)),
                pltpu.SemaphoreType.DMA((slots,)),
            ],
            compiler_params=pltpu.CompilerParams(vmem_limit_bytes=VMEM_LIMIT),
            cost_estimate=pl.CostEstimate(
                flops=2 * slots * slot_len * feat * 3 * bw,
                bytes_accessed=2 * feat * (3 * bw + slots * slot_len),
                transcendentals=0,
            ),
            name="attend_layer",
        )(ends_all, mod_slots[layer], *x_pieces, *qkv_pieces, *stale_slots[layer])
        plan = (slots, slot_len, cols, n_w, nr, bw, wc)
        shape = jax.ShapeDtypeStruct((slots, half, feat), jnp.bfloat16)
        keep, passed = pl.pallas_call(
            functools.partial(out_kernel, plan),
            out_shape=(shape, shape),
            in_specs=[vmem_spec()] + [any_spec()] * n_w,
            out_specs=(vmem_spec(), vmem_spec()),
            scratch_shapes=[
                pltpu.VMEM((feat, bw), jnp.bfloat16),
                pltpu.SemaphoreType.DMA((n_w,)),
            ],
            compiler_params=pltpu.CompilerParams(vmem_limit_bytes=VMEM_LIMIT),
            cost_estimate=pl.CostEstimate(
                flops=2 * slots * slot_len * feat * bw,
                bytes_accessed=2 * feat * (bw + slots * slot_len),
                transcendentals=0,
            ),
            name="project_out",
        )(attended, *out_pieces)
        chip_sum = keep.astype(jnp.float32) + to_core(passed).astype(jnp.float32)
        branch = jnp.zeros((half, wc), jnp.float32)
        for slot, di in enumerate(offsets):
            for dc in range(cols):
                part = chip_sum[slot, :, dc * wc : (dc + 1) * wc]
                if (di, dc) != (0, 0):
                    part = send_place(part.astype(jnp.bfloat16), di, dc).astype(jnp.float32)
                branch = branch + part
        gate_own = lax.dynamic_slice_in_dim(mod_layers[layer][2], c * wc, wc, 0)
        updated = x_half.astype(jnp.float32) + gate_own[None, :] * branch
        positions = jnp.arange(half)[:, None] + s * half
        return jnp.where(positions < ends[NP - 1], updated, 0.0).astype(jnp.bfloat16)

    x_half = lax.dynamic_slice_in_dim(hidden_in[0], s * half, half, 0)
    first = layer_step(0, gather(x_half), x_half)
    x_pieces = gather(first)
    second = layer_step(1, x_pieces, first)
    second_other = to_core(second)
    low = jnp.where(s == 0, first, second_other)
    high = jnp.where(s == 0, x_pieces[1], second)
    return jnp.concatenate([low, high], axis=0)[None, None]


def solution(mesh):
    return jax.shard_map(
        shards,
        mesh=mesh,
        in_specs=(
            P("row", None, "col"),
            P("row", None),
            P("row"),
            P("section", None, None, None),
            P("section", "row", None, "col"),
            P("section", "col", "row"),
            P("section", "row", None, "col"),
            P("section", "row", None, "col"),
        ),
        out_specs=P("section", "row", None, "col"),
        check_vma=False,
    )
```

time: 1050 us -> 458 us (0.44)
  waiting for transfers between devices: 644 us -> 300 us
  matrix products: 124 us -> 3.06 us
  local copies, waits for them, and re-layouts: 105 us -> 39.2 us
  other arithmetic: 74.7 us -> 13.8 us
  blocking collectives: 60.7 us -> 0 us
  starting transfers between devices: 7.22 us -> 51.5 us
  Pallas kernels: 0 us -> 41.9 us
  between operations: 21.7 us -> 1.76 us
    all_gather x2 -> x0, waiting for transfers between devices: 590 us -> none  [the longest x1 499 us: shards(): qkv_full = lax.all_gather(qkv_weight, 'row', axis=1, tiled=True)]
    ppermute x4 -> x59, waiting for transfers between devices: 1.17 us -> 300 us  [send_to(): return lax.ppermute(array, AXES, pairs)]
    dot_general x21 -> x1, matrix products: 124 us -> 3.06 us  [shards(): jnp.einsum('f,kfd->kd', embed_time(timestep)[0], mod_weight[0].transpose(...]
    reduce_scatter x5 -> x0, waiting for transfers between devices: 51.9 us -> none  [shards(): lax.psum_scatter(partial_out.astype(jnp.bfloat16), 'col', scatter_dimensi...]
    ppermute x4 -> x59, starting transfers between devices: 6.97 us -> 51.5 us  [send_to(): return lax.ppermute(array, AXES, pairs)]
    pallas_call x0 -> x4, Pallas kernels: none -> 41.9 us  [the longest x2 29.7 us: layer_step(): pl.pallas_call(functools.partial(attend_kernel, plan), out_shape=jax.Shap...]
    another operation x13 -> x6, other arithmetic: 40.9 us -> 2.76 us  [the longest x2 1.43 us: shards(): mod_slots = [jnp.stack([mod_both[l], mod_other[l]]) for l in range(2)]]
    scatter x15 -> x0, local copies, waits for them, and re-layouts: 35.2 us -> none  [update_one(): return lax.dynamic_update_slice_in_dim(source, new_rows, first_row, 0)]
  transfers between devices with their start and end apart: 11 -> 59, of which waited for: 10 -> 28; matrix products, arithmetic and copies ran while one was open for 9% -> 10% of each run, Pallas kernels for 0% -> 7%
where the time goes in v1:
time: 458 us; the launch traced here: 451 us
  waiting for transfers between devices  300 us (66%)
  starting transfers between devices  51.5 us (11%)
  Pallas kernels  41.9 us (9%)
  local copies, waits for them, and re-layouts  39.2 us (9%)
  other arithmetic  13.8 us (3%)
    ppermute x59, waiting for transfers between devices, send_to(): return lax.ppermute(array, AXES, pairs)  300 us
    ppermute x59, starting transfers between devices, send_to(): return lax.ppermute(array, AXES, pairs)  51.5 us
    pallas_call x2, Pallas kernels, layer_step(): pl.pallas_call(functools.partial(attend_kernel, plan), out_shape=jax.Shap...  29.7 us
    unnamed x114, local copies, waits for them, and re-layouts  12.6 us
    pallas_call x2, Pallas kernels, layer_step(): pl.pallas_call(functools.partial(out_kernel, plan), out_shape=(shape, sha...  12.2 us
  transfers between devices with their start and end apart: 59, of which 28 were waited for; matrix products, arithmetic and copies ran while one was open for 10% of the time, Pallas kernels for 7%

profile of v1, /device:TPU:0, one launch (start us, length us, event | category | flops | bytes accessed | tf_op | source)
XLA Modules:
  0.0 451.5 jit_solution(16975770276244223802)
XLA Ops:
  7.0 3.1 fusion
  11.3 6.9 %reshape.45 = bf16[3,384,2,2,384]{4,3,2,1,0:T(2,128)(2,1)S(1)} reshape(bf16[3,384,1536]{2,1,0:T(8,128)(2,1)} %bitcast.134) | data formatting | bytes 7077888 | tf_op jit(solution)/shard_map/reshape | solution.py:210
  18.3 3.7 constant_dynamic-slice_fusion.3
  26.1 3.2 stack.35
  37.8 20.8 %collective-permute-done.2 = f32[2,2,3072]{2,1,0:T(2,128)S(1)} collective-permute-done((f32[2,2,3072]{2,1,0:T(2,128)S(1)}, f32[2,2,3072]{2,1,0:T(2,128)S(1)}, u32[]{:S(2)}, u32[]{:S(2)}) %collective-permute-start.2) | collective-permute-done | bytes 49184 | tf_op jit(solution)/shard_map/ppermute | solution.py:26
  63.7 7.2 %collective-permute-done.6.refs_4_ = bf16[128,1536]{1,0:T(8,128)(2,1)} collective-permute-done((bf16[128,1536]{1,0:T(8,128)(2,1)}, bf16[128,1536]{1,0:T(8,128)(2,1)}, u32[]{:S(2)}, u32[]{:S(2)}) %collective-permute-start.6) | collective-permute-done | bytes 393248 | tf_op jit(solution)/shard_map/ppermute | solution.py:26
  74.4 11.5 %collective-permute-done.8.refs_6_ = bf16[128,1536]{1,0:T(8,128)(2,1)} collective-permute-done((bf16[128,1536]{1,0:T(8,128)(2,1)}, bf16[128,1536]{1,0:T(8,128)(2,1)}, u32[]{:S(2)}, u32[]{:S(2)}) %collective-permute-start.8) | collective-permute-done | bytes 393248 | tf_op jit(solution)/shard_map/ppermute | solution.py:26
  92.8 28.7 %collective-permute-done.22.refs_2_ = bf16[384,384]{1,0:T(8,128)(2,1)S(1)} collective-permute-done((bf16[384,384]{1,0:T(8,128)(2,1)S(1)}, bf16[384,384]{1,0:T(8,128)(2,1)S(1)}, u32[]{:S(2)}, u32[]{:S(2)}) %collective-permute-start.22) | collective-permute-done | bytes 294944 | tf_op jit(solution)/shard_map/ppermute | solution.py:26
  123.0 37.5 %collective-permute-done.24.refs_4_ = bf16[384,384]{1,0:T(8,128)(2,1)} collective-permute-done((bf16[384,384]{1,0:T(8,128)(2,1)S(1)}, bf16[384,384]{1,0:T(8,128)(2,1)}, u32[]{:S(2)}, u32[]{:S(2)}) %collective-permute-start.24) | collective-permute-done | bytes 294944 | tf_op jit(solution)/shard_map/ppermute | solution.py:26
  165.4 10.7 %collective-permute-done.26.refs_6_ = bf16[384,384]{1,0:T(8,128)(2,1)S(1)} collective-permute-done((bf16[384,384]{1,0:T(8,128)(2,1)S(1)}, bf16[384,384]{1,0:T(8,128)(2,1)S(1)}, u32[]{:S(2)}, u32[]{:S(2)}) %collective-permute-start.26) | collective-permute-done | bytes 294944 | tf_op jit(solution)/shard_map/ppermute | solution.py:26
  178.2 5.1 %collective-permute-done.13.refs_11_ = bf16[3,384,384]{2,1,0:T(8,128)(2,1)S(1)} collective-permute-done((bf16[3,384,384]{2,1,0:T(8,128)(2,1)}, bf16[3,384,384]{2,1,0:T(8,128)(2,1)S(1)}, u32[]{:S(2)}, u32[]{:S(2)}) %collective-permute-start.13) | collective-permute-done | bytes 884768 | tf_op jit(solution)/shard_map/ppermute | solution.py:26
  184.8 17.4 %collective-permute-done.15.refs_13_ = bf16[3,384,384]{2,1,0:T(8,128)(2,1)S(1)} collective-permute-done((bf16[3,384,384]{2,1,0:T(8,128)(2,1)S(1)}, bf16[3,384,384]{2,1,0:T(8,128)(2,1)S(1)}, u32[]{:S(2)}, u32[]{:S(2)}) %collective-permute-start.15) | collective-permute-done | bytes 884768 | tf_op jit(solution)/shard_map/ppermute | solution.py:26
  203.8 17.4 %collective-permute-done.17.refs_15_ = bf16[3,384,384]{2,1,0:T(8,128)(2,1)S(1)} collective-permute-done((bf16[3,384,384]{2,1,0:T(8,128)(2,1)S(1)}, bf16[3,384,384]{2,1,0:T(8,128)(2,1)S(1)}, u32[]{:S(2)}, u32[]{:S(2)}) %collective-permute-start.17) | collective-permute-done | bytes 884768 | tf_op jit(solution)/shard_map/ppermute | solution.py:26
  222.2 14.9 %attend_layer.2.attended_ref = bf16[512,384]{1,0:T(8,128)(2,1)} custom-call(s32[2,4]{1,0:T(2,128)} %pad_add_fusion.ends_ref, f32[2,2,3072]{2,1,0:T(2,128)} %pad_maximum_fusion.1.mod_ref, bf16[128,1536]{1,0:T(8,128)(2,1)} %dynamic-slice_bitcast_fusion.9.refs_0_, bf16[128,1536]{1,0:T(8,128)(2,1)} %collective-permute-done.3.refs_1_, ...), custom_call_target="tpu_custom_call" | custom-call | flops 3623878656 | bytes 10223616 | tf_op jit(solution)/shard_map/attend_layer/pallas_call | solution.py:293
  238.6 3.2 collective-permute-done.27.refs_7_
  242.5 6.1 %project_out.2 = (bf16[2,128,3072]{2,1,0:T(8,128)(2,1)}, bf16[2,128,3072]{2,1,0:T(8,128)(2,1)}) custom-call(bf16[512,384]{1,0:T(8,128)(2,1)} %attend_layer.2.attended_ref, bf16[384,384]{1,0:T(8,128)(2,1)} %copy-done.15, bf16[384,384]{1,0:T(8,128)(2,1)} %copy-done.47, bf16[384,384]{1,0:T(8,128)(2,1)} %copy-done.45, bf16[384,384]{1,0:T(8,128)(2,1)} %copy-done.49, ...), custom_call_target="tpu_custom_call" | custom-call | flops 1207959552 | bytes 5505024 | tf_op jit(solution)/shard_map/project_out/pallas_call | solution.py:318
  255.2 35.3 %collective-permute-done.40.refs_10_ = bf16[3,384,384]{2,1,0:T(8,128)(2,1)} collective-permute-done((bf16[3,384,384]{2,1,0:T(8,128)(2,1)S(1)}, bf16[3,384,384]{2,1,0:T(8,128)(2,1)}, u32[]{:S(2)}, u32[]{:S(2)}) %collective-permute-start.40) | collective-permute-done | bytes 884768 | tf_op jit(solution)/shard_map/ppermute | solution.py:26
  290.5 3.0 collective-permute-start.44
  295.3 3.6 collective-permute-done.46.refs_17_
  301.7 10.0 %collective-permute-done.48.refs_2_ = bf16[384,384]{1,0:T(8,128)(2,1)} collective-permute-done((bf16[384,384]{1,0:T(8,128)(2,1)S(1)}, bf16[384,384]{1,0:T(8,128)(2,1)}, u32[]{:S(2)}, u32[]{:S(2)}) %collective-permute-start.48) | collective-permute-done | bytes 294944 | tf_op jit(solution)/shard_map/ppermute | solution.py:26
  316.8 20.5 %collective-permute-done.44.refs_14_ = bf16[3,384,384]{2,1,0:T(8,128)(2,1)} collective-permute-done((bf16[3,384,384]{2,1,0:T(8,128)(2,1)}, bf16[3,384,384]{2,1,0:T(8,128)(2,1)}, u32[]{:S(2)}, u32[]{:S(2)}) %collective-permute-start.44) | collective-permute-done | bytes 884768 | tf_op jit(solution)/shard_map/ppermute | solution.py:26
  337.4 2.9 collective-permute-start.52
  344.3 16.3 %collective-permute-done.50.refs_4_ = bf16[384,384]{1,0:T(8,128)(2,1)} collective-permute-done((bf16[384,384]{1,0:T(8,128)(2,1)}, bf16[384,384]{1,0:T(8,128)(2,1)}, u32[]{:S(2)}, u32[]{:S(2)}) %collective-permute-start.50) | collective-permute-done | bytes 294944 | tf_op jit(solution)/shard_map/ppermute | solution.py:26
  361.1 5.3 %collective-permute-done.52.refs_6_ = bf16[384,384]{1,0:T(8,128)(2,1)} collective-permute-done((bf16[384,384]{1,0:T(8,128)(2,1)}, bf16[384,384]{1,0:T(8,128)(2,1)}, u32[]{:S(2)}, u32[]{:S(2)}) %collective-permute-start.52) | collective-permute-done | bytes 294944 | tf_op jit(solution)/shard_map/ppermute | solution.py:26
  370.7 7.7 %collective-permute-done.35.refs_4_ = bf16[128,1536]{1,0:T(8,128)(2,1)S(1)} collective-permute-done((bf16[128,1536]{1,0:T(8,128)(2,1)S(1)}, bf16[128,1536]{1,0:T(8,128)(2,1)S(1)}, u32[]{:S(2)}, u32[]{:S(2)}) %collective-permute-start.35) | collective-permute-done | bytes 393248 | tf_op jit(solution)/shard_map/ppermute | solution.py:26
  378.4 7.0 %collective-permute-done.37.refs_6_ = bf16[128,1536]{1,0:T(8,128)(2,1)S(1)} collective-permute-done((bf16[128,1536]{1,0:T(8,128)(2,1)S(1)}, bf16[128,1536]{1,0:T(8,128)(2,1)S(1)}, u32[]{:S(2)}, u32[]{:S(2)}) %collective-permute-start.37) | collective-permute-done | bytes 393248 | tf_op jit(solution)/shard_map/ppermute | solution.py:26
  391.1 14.9 %attend_layer.3.attended_ref = bf16[512,384]{1,0:T(8,128)(2,1)} custom-call(s32[2,4]{1,0:T(2,128)} %pad_add_fusion.ends_ref, f32[2,2,3072]{2,1,0:T(2,128)} %pad_maximum_fusion.2.mod_ref, bf16[128,1536]{1,0:T(8,128)(2,1)} %copy-done.2, bf16[128,1536]{1,0:T(8,128)(2,1)} %copy-done.10, bf16[128,1536]{1,0:T(8,128)(2,1)} %copy-done.39, ...), custom_call_target="tpu_custom_call" | custom-call | flops 3623878656 | bytes 10223616 | tf_op jit(solution)/shard_map/attend_layer/pallas_call | solution.py:293
  408.7 5.8 %collective-permute-done.53.refs_7_ = bf16[384,384]{1,0:T(8,128)(2,1)S(1)} collective-permute-done((bf16[384,384]{1,0:T(8,128)(2,1)}, bf16[384,384]{1,0:T(8,128)(2,1)S(1)}, u32[]{:S(2)}, u32[]{:S(2)}) %collective-permute-start.53) | collective-permute-done | bytes 294944 | tf_op jit(solution)/shard_map/ppermute | solution.py:26
  415.3 6.1 %project_out.3 = (bf16[2,128,3072]{2,1,0:T(8,128)(2,1)}, bf16[2,128,3072]{2,1,0:T(8,128)(2,1)}) custom-call(bf16[512,384]{1,0:T(8,128)(2,1)} %attend_layer.3.attended_ref, bf16[384,384]{1,0:T(8,128)(2,1)} %get-tuple-element.21.refs_0_, bf16[384,384]{1,0:T(8,128)(2,1)} %copy-done.48, bf16[384,384]{1,0:T(8,128)(2,1)} %collective-permute-done.48.refs_2_, ...), custom_call_target="tpu_custom_call" | custom-call | flops 1207959552 | bytes 5505024 | tf_op jit(solution)/shard_map/project_out/pallas_call | solution.py:318
  421.5 3.6 collective-permute-done.54
  431.7 8.6 %collective-permute-done.57 = bf16[128,1536]{1,0:T(8,128)(2,1)S(1)} collective-permute-done((bf16[128,1536]{1,0:T(8,128)(2,1)S(1)}, bf16[128,1536]{1,0:T(8,128)(2,1)S(1)}, u32[]{:S(2)}, u32[]{:S(2)}) %collective-permute-start.57) | collective-permute-done | bytes 393248 | tf_op jit(solution)/shard_map/ppermute | solution.py:26
  440.2 7.7 %collective-permute-done.56 = bf16[128,1536]{1,0:T(8,128)(2,1)S(1)} collective-permute-done((bf16[128,1536]{1,0:T(8,128)(2,1)S(1)}, bf16[128,1536]{1,0:T(8,128)(2,1)S(1)}, u32[]{:S(2)}, u32[]{:S(2)}) %collective-permute-start.56) | collective-permute-done | bytes 393248 | tf_op jit(solution)/shard_map/ppermute | solution.py:26
  (248 shorter events, 94.1 us)
Async XLA Ops:
  1.8 57.3 %collective-permute-start.3 = (bf16[128,1536]{1,0:T(8,128)(2,1)}, bf16[128,1536]{1,0:T(8,128)(2,1)}, u32[]{:S(2)}, u32[]{:S(2)}) collective-permute-start(bf16[128,1536]{1,0:T(8,128)(2,1)} %dynamic-slice_bitcast_fusion.9.refs_0_), channel_id=1, source_target_pairs={{0,16},{1,17},{2,18},{3,19},{4,20},{5,21},{6,22},{7,23},{8,24},{9,... | collective-permute-start | bytes 1179656 | tf_op jit(solution)/shard_map/ppermute | solution.py:26
  2.2 59.3 %collective-permute-start.4 = (bf16[128,1536]{1,0:T(8,128)(2,1)}, bf16[128,1536]{1,0:T(8,128)(2,1)}, u32[]{:S(2)}, u32[]{:S(2)}) collective-permute-start(bf16[128,1536]{1,0:T(8,128)(2,1)} %dynamic-slice_bitcast_fusion.9.refs_0_), channel_id=1, source_target_pairs={{0,1},{1,0},{2,3},{3,2},{4,5},{5,4},{6,7},{7,6},{8,9},{9,8},{10,11... | collective-permute-start | bytes 1179656 | tf_op jit(solution)/shard_map/ppermute | solution.py:26
  4.7 31.2 %collective-permute-start.1 = (s32[4]{0:T(128)}, s32[4]{0:T(128)S(1)}, u32[]{:S(2)}, u32[]{:S(2)}) collective-permute-start(s32[4]{0:T(128)} %bitcast.136), channel_id=1, source_target_pairs={{0,4},{1,5},{2,6},{3,7},{4,0},{5,1},{6,2},{7,3},{8,12},{9,13},{10,... | collective-permute-start | bytes 56 | tf_op jit(solution)/shard_map/ppermute | solution.py:26
  30.4 55.5 %collective-permute-start.20 = (bf16[2,384,384]{2,1,0:T(8,128)(2,1)}, bf16[2,384,384]{2,1,0:T(8,128)(2,1)}, u32[]{:S(2)}, u32[]{:S(2)}) collective-permute-start(bf16[2,384,384]{2,1,0:T(8,128)(2,1)} %bitcast.28), channel_id=1, source_target_pairs={{0,16},{1,17},{2,18},{3,19},{4,20},{5,21},{6,22},{7,23},{8,24},{9,... | collective-permute-start | bytes 1769480 | tf_op jit(solution)/shard_map/ppermute | solution.py:26
  35.4 38.1 %collective-permute-start.12 = (bf16[3,384,384]{2,1,0:T(8,128)(2,1)}, bf16[3,384,384]{2,1,0:T(8,128)(2,1)}, u32[]{:S(2)}, u32[]{:S(2)}) collective-permute-start(bf16[3,384,384]{2,1,0:T(8,128)(2,1)} %get-tuple-element.39), channel_id=1, source_target_pairs={{0,4},{1,5},{2,6},{3,7},{4,0},{5,1},{6,2},{7,3},{8,12},{9,13},{10,... | collective-permute-start | bytes 2654216 | tf_op jit(solution)/shard_map/ppermute | solution.py:26
  59.0 26.9 %collective-permute-start.8 = (bf16[128,1536]{1,0:T(8,128)(2,1)}, bf16[128,1536]{1,0:T(8,128)(2,1)}, u32[]{:S(2)}, u32[]{:S(2)}) collective-permute-start(bf16[128,1536]{1,0:T(8,128)(2,1)} %dynamic-slice_bitcast_fusion.9.refs_0_), channel_id=1, source_target_pairs={{0,5},{1,4},{2,7},{3,6},{4,1},{5,0},{6,3},{7,2},{8,13},{9,12},{10,... | collective-permute-start | bytes 1179656 | tf_op jit(solution)/shard_map/ppermute | solution.py:26
  61.5 26.9 %collective-permute-start.18 = (bf16[2,2,256,384]{3,2,1,0:T(8,128)(2,1)}, bf16[2,2,256,384]{3,2,1,0:T(8,128)(2,1)}, u32[]{:S(2)}, u32[]{:S(2)}) collective-permute-start(bf16[2,2,256,384]{3,2,1,0:T(8,128)(2,1)} %dynamic-slice_bitcast_fusion.4), channel_id=1, source_target_pairs={{0,16},{1,17},{2,18},{3,19},{4,20},{5,21},{6,22},{7,23},{8,24},{9,... | collective-permute-start | bytes 2359304 | tf_op jit(solution)/shard_map/ppermute | solution.py:26
  70.9 91.1 %collective-permute-start.14 = (bf16[3,384,384]{2,1,0:T(8,128)(2,1)}, bf16[3,384,384]{2,1,0:T(8,128)(2,1)S(1)}, u32[]{:S(2)}, u32[]{:S(2)}) collective-permute-start(bf16[3,384,384]{2,1,0:T(8,128)(2,1)} %get-tuple-element.40.refs_8_), channel_id=1, source_target_pairs={{0,8},{1,9},{2,10},{3,11},{4,12},{5,13},{6,14},{7,15},{8,0},{9,1},... | collective-permute-start | bytes 2654216 | tf_op jit(solution)/shard_map/ppermute | solution.py:26
  73.5 89.1 %collective-permute-start.16 = (bf16[3,384,384]{2,1,0:T(8,128)(2,1)}, bf16[3,384,384]{2,1,0:T(8,128)(2,1)S(1)}, u32[]{:S(2)}, u32[]{:S(2)}) collective-permute-start(bf16[3,384,384]{2,1,0:T(8,128)(2,1)} %collective-permute-done.12.refs_10_), channel_id=1, source_target_pairs={{0,8},{1,9},{2,10},{3,11},{4,12},{5,13},{6,14},{7,15},{8,0},{9,1},... | collective-permute-start | bytes 2654216 | tf_op jit(solution)/shard_map/ppermute | solution.py:26
  88.4 33.1 %collective-permute-start.22 = (bf16[384,384]{1,0:T(8,128)(2,1)S(1)}, bf16[384,384]{1,0:T(8,128)(2,1)S(1)}, u32[]{:S(2)}, u32[]{:S(2)}) collective-permute-start(bf16[384,384]{1,0:T(8,128)(2,1)S(1)} %get-tuple-element.57), channel_id=1, source_target_pairs={{0,4},{1,5},{2,6},{3,7},{4,0},{5,1},{6,2},{7,3},{8,12},{9,13},{10,... | collective-permute-start | bytes 884744 | tf_op jit(solution)/shard_map/ppermute | solution.py:26
  89.2 71.3 %collective-permute-start.24 = (bf16[384,384]{1,0:T(8,128)(2,1)S(1)}, bf16[384,384]{1,0:T(8,128)(2,1)}, u32[]{:S(2)}, u32[]{:S(2)}) collective-permute-start(bf16[384,384]{1,0:T(8,128)(2,1)S(1)} %get-tuple-element.58.refs_0_), channel_id=1, source_target_pairs={{0,8},{1,9},{2,10},{3,11},{4,12},{5,13},{6,14},{7,15},{8,0},{9,1},... | collective-permute-start | bytes 884744 | tf_op jit(solution)/shard_map/ppermute | solution.py:26
  91.5 73.2 %collective-permute-start.19 = (bf16[2,256,384]{2,1,0:T(8,128)(2,1)S(1)}, bf16[2,256,384]{2,1,0:T(8,128)(2,1)S(1)}, u32[]{:S(2)}, u32[]{:S(2)}) collective-permute-start(bf16[2,256,384]{2,1,0:T(8,128)(2,1)S(1)} %get-tuple-element.53), channel_id=1, source_target_pairs={{0,4},{1,5},{2,6},{3,7},{4,0},{5,1},{6,2},{7,3},{8,12},{9,13},{10,... | collective-permute-start | bytes 1179656 | tf_op jit(solution)/shard_map/ppermute | solution.py:26
  121.5 55.2 %collective-permute-start.11 = (bf16[3,384,384]{2,1,0:T(8,128)(2,1)S(1)}, bf16[3,384,384]{2,1,0:T(8,128)(2,1)S(1)}, u32[]{:S(2)}, u32[]{:S(2)}) collective-permute-start(bf16[3,384,384]{2,1,0:T(8,128)(2,1)S(1)} %copy-done.8), channel_id=1, source_target_pairs={{0,2},{1,3},{2,0},{3,1},{4,6},{5,7},{6,4},{7,5},{8,10},{9,11},{10,... | collective-permute-start | bytes 2654216 | tf_op jit(solution)/shard_map/ppermute | solution.py:26
  162.1 40.2 %collective-permute-start.15 = (bf16[3,384,384]{2,1,0:T(8,128)(2,1)S(1)}, bf16[3,384,384]{2,1,0:T(8,128)(2,1)S(1)}, u32[]{:S(2)}, u32[]{:S(2)}) collective-permute-start(bf16[3,384,384]{2,1,0:T(8,128)(2,1)S(1)} %collective-permute-done.14.refs_12_), channel_id=1, source_target_pairs={{0,2},{1,3},{2,0},{3,1},{4,6},{5,7},{6,4},{7,5},{8,10},{9,11},{10,... | collective-permute-start | bytes 2654216 | tf_op jit(solution)/shard_map/ppermute | solution.py:26
  162.6 58.7 %collective-permute-start.17 = (bf16[3,384,384]{2,1,0:T(8,128)(2,1)S(1)}, bf16[3,384,384]{2,1,0:T(8,128)(2,1)S(1)}, u32[]{:S(2)}, u32[]{:S(2)}) collective-permute-start(bf16[3,384,384]{2,1,0:T(8,128)(2,1)S(1)} %collective-permute-done.16.refs_14_), channel_id=1, source_target_pairs={{0,2},{1,3},{2,0},{3,1},{4,6},{5,7},{6,4},{7,5},{8,10},{9,11},{10,... | collective-permute-start | bytes 2654216 | tf_op jit(solution)/shard_map/ppermute | solution.py:26
  176.1 61.0 %collective-permute-start.21 = (bf16[384,384]{1,0:T(8,128)(2,1)S(1)}, bf16[384,384]{1,0:T(8,128)(2,1)S(1)}, u32[]{:S(2)}, u32[]{:S(2)}) collective-permute-start(bf16[384,384]{1,0:T(8,128)(2,1)S(1)} %get-tuple-element.58.refs_0_), channel_id=1, source_target_pairs={{0,2},{1,3},{2,0},{3,1},{4,6},{5,7},{6,4},{7,5},{8,10},{9,11},{10,... | collective-permute-start | bytes 884744 | tf_op jit(solution)/shard_map/ppermute | solution.py:26
  176.7 60.4 %collective-permute-start.23 = (bf16[384,384]{1,0:T(8,128)(2,1)S(1)}, bf16[384,384]{1,0:T(8,128)(2,1)S(1)}, u32[]{:S(2)}, u32[]{:S(2)}) collective-permute-start(bf16[384,384]{1,0:T(8,128)(2,1)S(1)} %collective-permute-done.22.refs_2_), channel_id=1, source_target_pairs={{0,2},{1,3},{2,0},{3,1},{4,6},{5,7},{6,4},{7,5},{8,10},{9,11},{10,... | collective-permute-start | bytes 884744 | tf_op jit(solution)/shard_map/ppermute | solution.py:26
  183.3 55.3 %collective-permute-start.25 = (bf16[384,384]{1,0:T(8,128)(2,1)}, bf16[384,384]{1,0:T(8,128)(2,1)S(1)}, u32[]{:S(2)}, u32[]{:S(2)}) collective-permute-start(bf16[384,384]{1,0:T(8,128)(2,1)} %collective-permute-done.24.refs_4_), channel_id=1, source_target_pairs={{0,2},{1,3},{2,0},{3,1},{4,6},{5,7},{6,4},{7,5},{8,10},{9,11},{10,... | collective-permute-start | bytes 884744 | tf_op jit(solution)/shard_map/ppermute | solution.py:26
  202.3 39.5 %collective-permute-start.27 = (bf16[384,384]{1,0:T(8,128)(2,1)S(1)}, bf16[384,384]{1,0:T(8,128)(2,1)S(1)}, u32[]{:S(2)}, u32[]{:S(2)}) collective-permute-start(bf16[384,384]{1,0:T(8,128)(2,1)S(1)} %collective-permute-done.26.refs_6_), channel_id=1, source_target_pairs={{0,2},{1,3},{2,0},{3,1},{4,6},{5,7},{6,4},{7,5},{8,10},{9,11},{10,... | collective-permute-start | bytes 884744 | tf_op jit(solution)/shard_map/ppermute | solution.py:26
  248.7 41.9 %collective-permute-start.28 = (bf16[2,128,3072]{2,1,0:T(8,128)(2,1)}, bf16[2,128,3072]{2,1,0:T(8,128)(2,1)S(1)}, u32[]{:S(2)}, u32[]{:S(2)}) collective-permute-start(bf16[2,128,3072]{2,1,0:T(8,128)(2,1)} %get-tuple-element.16), channel_id=1, source_target_pairs={{0,16},{1,17},{2,18},{3,19},{4,20},{5,21},{6,22},{7,23},{8,24},{9,... | collective-permute-start | bytes 4718600 | tf_op jit(solution)/shard_map/ppermute | solution.py:26
  248.9 41.6 %collective-permute-start.40 = (bf16[3,384,384]{2,1,0:T(8,128)(2,1)S(1)}, bf16[3,384,384]{2,1,0:T(8,128)(2,1)}, u32[]{:S(2)}, u32[]{:S(2)}) collective-permute-start(bf16[3,384,384]{2,1,0:T(8,128)(2,1)S(1)} %get-tuple-element.17), channel_id=1, source_target_pairs={{0,4},{1,5},{2,6},{3,7},{4,0},{5,1},{6,2},{7,3},{8,12},{9,13},{10,... | collective-permute-start | bytes 2654216 | tf_op jit(solution)/shard_map/ppermute | solution.py:26
  250.7 48.3 %collective-permute-start.46 = (bf16[2,256,384]{2,1,0:T(8,128)(2,1)S(1)}, bf16[2,256,384]{2,1,0:T(8,128)(2,1)S(1)}, u32[]{:S(2)}, u32[]{:S(2)}) collective-permute-start(bf16[2,256,384]{2,1,0:T(8,128)(2,1)S(1)} %get-tuple-element.51), channel_id=1, source_target_pairs={{0,4},{1,5},{2,6},{3,7},{4,0},{5,1},{6,2},{7,3},{8,12},{9,13},{10,... | collective-permute-start | bytes 1179656 | tf_op jit(solution)/shard_map/ppermute | solution.py:26
  252.7 47.0 %collective-permute-start.39 = (bf16[3,384,384]{2,1,0:T(8,128)(2,1)S(1)}, bf16[3,384,384]{2,1,0:T(8,128)(2,1)S(1)}, u32[]{:S(2)}, u32[]{:S(2)}) collective-permute-start(bf16[3,384,384]{2,1,0:T(8,128)(2,1)S(1)} %get-tuple-element.18.refs_8_), channel_id=1, source_target_pairs={{0,2},{1,3},{2,0},{3,1},{4,6},{5,7},{6,4},{7,5},{8,10},{9,11},{10,... | collective-permute-start | bytes 2654216 | tf_op jit(solution)/shard_map/ppermute | solution.py:26
  254.2 58.0 %collective-permute-start.42 = (bf16[3,384,384]{2,1,0:T(8,128)(2,1)S(1)}, bf16[3,384,384]{2,1,0:T(8,128)(2,1)S(1)}, u32[]{:S(2)}, u32[]{:S(2)}) collective-permute-start(bf16[3,384,384]{2,1,0:T(8,128)(2,1)S(1)} %get-tuple-element.18.refs_8_), channel_id=1, source_target_pairs={{0,8},{1,9},{2,10},{3,11},{4,12},{5,13},{6,14},{7,15},{8,0},{9,1},... | collective-permute-start | bytes 2654216 | tf_op jit(solution)/shard_map/ppermute | solution.py:26
  290.5 46.8 %collective-permute-start.44 = (bf16[3,384,384]{2,1,0:T(8,128)(2,1)}, bf16[3,384,384]{2,1,0:T(8,128)(2,1)}, u32[]{:S(2)}, u32[]{:S(2)}) collective-permute-start(bf16[3,384,384]{2,1,0:T(8,128)(2,1)} %collective-permute-done.40.refs_10_), channel_id=1, source_target_pairs={{0,8},{1,9},{2,10},{3,11},{4,12},{5,13},{6,14},{7,15},{8,0},{9,1},... | collective-permute-start | bytes 2654216 | tf_op jit(solution)/shard_map/ppermute | solution.py:26
  299.7 37.7 %collective-permute-start.31 = (bf16[128,1536]{1,0:T(8,128)(2,1)}, bf16[128,1536]{1,0:T(8,128)(2,1)S(1)}, u32[]{:S(2)}, u32[]{:S(2)}) collective-permute-start(bf16[128,1536]{1,0:T(8,128)(2,1)} %get-tuple-element.45), channel_id=1, source_target_pairs={{0,5},{1,4},{2,7},{3,6},{4,1},{5,0},{6,3},{7,2},{8,13},{9,12},{10,... | collective-permute-start | bytes 1179656 | tf_op jit(solution)/shard_map/ppermute | solution.py:26
  299.7 41.0 %collective-permute-start.30 = (bf16[128,1536]{1,0:T(8,128)(2,1)}, bf16[128,1536]{1,0:T(8,128)(2,1)}, u32[]{:S(2)}, u32[]{:S(2)}) collective-permute-start(bf16[128,1536]{1,0:T(8,128)(2,1)} %get-tuple-element.46), channel_id=1, source_target_pairs={{0,4},{1,5},{2,6},{3,7},{4,0},{5,1},{6,2},{7,3},{8,12},{9,13},{10,... | collective-permute-start | bytes 1179656 | tf_op jit(solution)/shard_map/ppermute | solution.py:26
  311.7 30.6 %collective-permute-start.29 = (bf16[128,1536]{1,0:T(8,128)(2,1)}, bf16[128,1536]{1,0:T(8,128)(2,1)}, u32[]{:S(2)}, u32[]{:S(2)}) collective-permute-start(bf16[128,1536]{1,0:T(8,128)(2,1)} %get-tuple-element.44), channel_id=1, source_target_pairs={{0,1},{1,0},{2,3},{3,2},{4,5},{5,4},{6,7},{7,6},{8,9},{9,8},{10,11... | collective-permute-start | bytes 1179656 | tf_op jit(solution)/shard_map/ppermute | solution.py:26
  313.2 53.2 %collective-permute-start.41 = (bf16[3,384,384]{2,1,0:T(8,128)(2,1)}, bf16[3,384,384]{2,1,0:T(8,128)(2,1)}, u32[]{:S(2)}, u32[]{:S(2)}) collective-permute-start(bf16[3,384,384]{2,1,0:T(8,128)(2,1)} %collective-permute-done.40.refs_10_), channel_id=1, source_target_pairs={{0,2},{1,3},{2,0},{3,1},{4,6},{5,7},{6,4},{7,5},{8,10},{9,11},{10,... | collective-permute-start | bytes 2654216 | tf_op jit(solution)/shard_map/ppermute | solution.py:26
  337.4 29.0 %collective-permute-start.52 = (bf16[384,384]{1,0:T(8,128)(2,1)}, bf16[384,384]{1,0:T(8,128)(2,1)}, u32[]{:S(2)}, u32[]{:S(2)}) collective-permute-start(bf16[384,384]{1,0:T(8,128)(2,1)} %collective-permute-done.48.refs_2_), channel_id=1, source_target_pairs={{0,8},{1,9},{2,10},{3,11},{4,12},{5,13},{6,14},{7,15},{8,0},{9,1},... | collective-permute-start | bytes 884744 | tf_op jit(solution)/shard_map/ppermute | solution.py:26
  340.7 27.7 %collective-permute-start.43 = (bf16[3,384,384]{2,1,0:T(8,128)(2,1)}, bf16[3,384,384]{2,1,0:T(8,128)(2,1)S(1)}, u32[]{:S(2)}, u32[]{:S(2)}) collective-permute-start(bf16[3,384,384]{2,1,0:T(8,128)(2,1)} %copy-done.25), channel_id=1, source_target_pairs={{0,2},{1,3},{2,0},{3,1},{4,6},{5,7},{6,4},{7,5},{8,10},{9,11},{10,... | collective-permute-start | bytes 2654216 | tf_op jit(solution)/shard_map/ppermute | solution.py:26
  342.2 43.9 %collective-permute-start.45 = (bf16[3,384,384]{2,1,0:T(8,128)(2,1)}, bf16[3,384,384]{2,1,0:T(8,128)(2,1)S(1)}, u32[]{:S(2)}, u32[]{:S(2)}) collective-permute-start(bf16[3,384,384]{2,1,0:T(8,128)(2,1)} %collective-permute-done.44.refs_14_), channel_id=1, source_target_pairs={{0,2},{1,3},{2,0},{3,1},{4,6},{5,7},{6,4},{7,5},{8,10},{9,11},{10,... | collective-permute-start | bytes 2654216 | tf_op jit(solution)/shard_map/ppermute | solution.py:26
  (82 other events, 1680.3 us)

commit v2 on v1

--- a/solution.py
+++ b/solution.py
@@ -62,7 +62,7 @@
 def attend_kernel(plan, ends_ref, mod_ref, *refs):
     slots, slot_len, cols, n_x, n_w, kr, bw, wc = plan
     x_refs, refs = refs[:n_x], refs[n_x:]
-    w_refs, refs = refs[:n_w], refs[n_w:]
+    w_refs, refs = refs[: 3 * n_w], refs[3 * n_w :]
     kv_refs, refs = refs[:slots], refs[slots:]
     out_ref, xv, xm, wv, kvv, x_sem, w_sem, kv_sem = refs
     s, i, c = (lax.axis_index(axis) for axis in AXES)
@@ -83,7 +83,10 @@
                 place += 1
     for d in range(n_w):
         rows = pl.ds(pl.multiple_of((i ^ d) * kr, 32), kr)
-        w_copies.append(pltpu.make_async_copy(w_refs[d], wv.at[:, rows, :], w_sem.at[d]))
+        for t in range(3):
+            w_copies.append(
+                pltpu.make_async_copy(w_refs[3 * d + t], wv.at[t, rows, :], w_sem.at[3 * d + t])
+            )
     for slot in range(slots):
         kv_copies.append(pltpu.make_async_copy(kv_refs[slot], kvv.at[slot], kv_sem.at[slot]))
     for copy in x_copies + w_copies + kv_copies:
@@ -160,32 +163,85 @@
     o_refs, refs = refs[:n_w], refs[n_w:]
     keep_ref, pass_ref, ov, o_sem = refs
     s, i, c = (lax.axis_index(axis) for axis in AXES)
-    feat = cols * wc
     half = slot_len // 2
     copies = []
     for d in range(n_w):
-        start = lax.rem((i ^ d) * nr + feat - c * wc, feat)
-        rows = pl.ds(pl.multiple_of(start, 32), nr)
-        copies.append(pltpu.make_async_copy(o_refs[d], ov.at[rows, :], o_sem.at[d]))
+        place = lax.rem((i ^ d) + n_w - c * (n_w // cols), n_w)
+        copies.append(pltpu.make_async_copy(o_refs[d], ov.at[place], o_sem.at[d]))
     for copy in copies:
         copy.start()
     for copy in copies:
         copy.wait()
-    contract = (((1,), (1,)), ((), ()))
     blocks = []
     for side in (s, 1 - s):
         for slot in range(slots):
             row = pl.multiple_of(slot * slot_len + side * half, half)
             blocks.append(attended_ref[pl.ds(row, half), :])
     lhs = jnp.concatenate(blocks, axis=0)
-    tile = wc // 3
-    for first in range(0, feat, tile):
-        part = lax.dot_general(
-            lhs, ov[first : first + tile, :], contract, preferred_element_type=jnp.float32
-        ).astype(jnp.bfloat16)
-        part = part.reshape(2, slots, half, tile)
-        keep_ref[:, :, first : first + tile] = part[0]
-        pass_ref[:, :, first : first + tile] = part[1]
+    for place in range(n_w):
+        part = jnp.dot(lhs, ov[place], preferred_element_type=jnp.float32).astype(jnp.bfloat16)
+        part = part.reshape(2, slots, half, nr)
+        lanes = slice(place * nr, (place + 1) * nr)
+        keep_ref[:, :, lanes] = part[0]
+        pass_ref[:, :, lanes] = part[1]
+
+
+def split_kernel(plan, *refs):
+    slots, bw = plan
+    qkv_ref, o_ref, key_ref, value_ref = refs[:4]
+    outs, sem = refs[4:-1], refs[-1]
+    s, i = lax.axis_index("section"), lax.axis_index("row")
+    mine_at = lax.rem(i // 2, 2) if slots == 2 else 0
+    copies = []
+    for kind in range(5):
+        for side, core in enumerate((1 - s, s)):
+            for slot in range(slots):
+                block = core * slots + (mine_at if slot == 0 else 1 - mine_at)
+                span = pl.ds(pl.multiple_of(block * bw, 128), bw)
+                out = outs[2 * kind + side]
+                if kind < 3:
+                    pairs = [(qkv_ref.at[kind, :, span], out.at[slot])]
+                elif kind == 3:
+                    pairs = [(o_ref.at[span, :], out.at[slot])]
+                else:
+                    pairs = [
+                        (ref.at[:, span], out.at[slot, t])
+                        for t, ref in enumerate((key_ref, value_ref))
+                    ]
+                for source, target in pairs:
+                    one = pltpu.make_async_copy(source, target, sem.at[len(copies)])
+                    one.start()
+                    copies.append(one)
+    for one in copies:
+        one.wait()
+
+
+def choose_kernel(plan, *refs):
+    slots, layer, kinds = plan
+    pairs, outs, sem = refs[: 2 * kinds], refs[2 * kinds : -1], refs[-1]
+    s = lax.axis_index("section")
+    for side, mine in enumerate((s == layer, s != layer)):
+
+        @pl.when(mine)
+        def _(side=side):
+            copies = []
+            for kind in range(kinds):
+                for slot in range(slots):
+                    place = kind * slots + slot
+                    one = pltpu.make_async_copy(
+                        pairs[2 * kind + side].at[slot], outs[place], sem.at[place]
+                    )
+                    one.start()
+                    copies.append(one)
+            for one in copies:
+                one.wait()
+
+
+def mod_kernel(slots, feats_ref, weight_ref, out_ref):
+    for k in range(3):
+        part = jnp.dot(feats_ref[...], weight_ref[k], preferred_element_type=jnp.float32)
+        for slot in range(slots):
+            out_ref[slot, k : k + 1, :] = part[slot : slot + 1, :]
 
 
 def shards(
@@ -203,98 +259,111 @@
     row_bits = [1 << b for b in range(rows.bit_length() - 1)]
     split_bit = 2 if slots == 2 else 0
     group_bits = [b for b in reversed(row_bits) if b != split_bit]
-    mine_at = (i // 2) % 2 if slots == 2 else 0
     offsets = [0, split_bit] if slots == 2 else [0]
-
-    qkv_blocks = jnp.transpose(
-        qkv_weight[0].transpose(1, 0, 2).reshape(3, kr, sections, slots, bw), (2, 3, 0, 1, 4)
-    )
-    out_blocks = out_weight[0].reshape(sections, slots, bw, nr).transpose(0, 1, 3, 2)
-    stale = jnp.stack([stale_keys[0, 0], stale_values[0, 0]])
-    stale_blocks = stale.reshape(2, slot_len, sections, slots, bw).transpose(2, 3, 0, 1, 4)
-
-    def both_layers(blocks):
-        own, other = pick(blocks, s), to_core(pick(blocks, 1 - s))
-        return jnp.where(s == 0, own, other), jnp.where(s == 0, other, own)
-
-    qkv_layers = both_layers(qkv_blocks)
-    out_layers = both_layers(out_blocks)
-    stale_layers = both_layers(stale_blocks)
-
-    modulation = jnp.einsum(
-        "f,kfd->kd",
-        embed_time(timestep)[0],
-        mod_weight[0].transpose(1, 0, 2),
-        preferred_element_type=jnp.float32,
-    )
-    other_modulation = to_core(modulation)
-    mod_layers = (
-        jnp.where(s == 0, modulation, other_modulation),
-        jnp.where(s == 0, other_modulation, modulation),
-    )
-    ends = patch_ends[0]
-    if slots == 2:
-        ends_all = jnp.stack([ends, to_row(ends, split_bit)])
-        mod_both = jnp.stack([mod_layers[0][:2], mod_layers[1][:2]])
-        mod_other = to_row(mod_both, split_bit)
-        mod_slots = [jnp.stack([mod_both[l], mod_other[l]]) for l in range(2)]
-    else:
-        ends_all = ends[None]
-        mod_slots = [mod_layers[l][:2][None] for l in range(2)]
-
-    def spread(own, gate):
-        pieces = {0: pick(own, mine_at)}
-        if slots == 2:
-            sent = pick(own, 1 - mine_at)
-            pieces[split_bit] = to_row(after(sent, *gate) if gate else sent, split_bit)
-        crossed = []
-        for bit in group_bits:
-            new = {}
-            for d, piece in pieces.items():
-                if bit == group_bits[0] and gate:
-                    piece = after(piece, *gate)
-                new[d ^ bit] = to_row(piece, bit)
-            if bit == group_bits[0]:
-                crossed = list(new.values())
-            pieces.update(new)
-        return [pieces[d] for d in range(rows)], crossed
-
-    qkv0, gate_q = spread(qkv_layers[0], ())
-    out0, gate_o = spread(out_layers[0], ())
-    gate = gate_q + gate_o
-    qkv1, gate_q = spread(qkv_layers[1], gate)
-    out1, _ = spread(out_layers[1], gate)
-    weights = ((qkv0, out0), (qkv1, out1))
-
-    stale_slots = []
-    for layer in range(2):
-        own = stale_layers[layer]
-        block = [pick(own, mine_at)]
-        if slots == 2:
-            block.append(to_row(pick(own, 1 - mine_at), split_bit))
-        stale_slots.append(block)
 
     places = [(di, dc) for di in offsets for dc in range(cols)]
 
     def send_place(array, di, dc):
         return send_to(array, lambda si, ii, ci: (si, ii ^ di, (ci + dc) % cols))
 
-    def gather(own_half):
-        pieces = []
-        for di, dc in places:
-            got = own_half if (di, dc) == (0, 0) else send_place(own_half, di, dc)
-            pieces.extend([got, to_core(got)])
-        return pieces
-
-    def layer_step(layer, x_pieces, x_half):
-        qkv_pieces, out_pieces = weights[layer]
-        n_w = rows
-        plan = (slots, slot_len, cols, len(x_pieces), n_w, kr, bw, wc)
-        attended = pl.pallas_call(
+    def gather_chips(own_half):
+        return [own_half if p == (0, 0) else send_place(own_half, *p) for p in places]
+
+    def gather(pieces):
+        return [one for piece in pieces for one in (piece, to_core(piece))]
+
+    numbers = jnp.concatenate([patch_ends[0], timestep])
+    numbers = jnp.stack([numbers] + [to_row(numbers, bit) for bit in offsets[1:]])
+    ends_all, steps = numbers[:, :NP], numbers[:, NP]
+    x_half = lax.dynamic_slice_in_dim(hidden_in[0], s * half, half, 0)
+    x_chips = gather_chips(x_half)
+
+    shapes = [(kr, bw)] * 3 + [(bw, nr), (2, slot_len, bw)]
+    shapes = [jax.ShapeDtypeStruct(shape, jnp.bfloat16) for shape in shapes]
+    stacked = [jax.ShapeDtypeStruct((slots,) + b.shape, b.dtype) for b in shapes]
+    cut = pl.pallas_call(
+        functools.partial(split_kernel, (slots, bw)),
+        out_shape=[b for b in stacked for _ in range(2)],
+        in_specs=[any_spec()] * 4,
+        out_specs=[any_spec()] * 10,
+        scratch_shapes=[pltpu.SemaphoreType.DMA((12 * slots,))],
+        compiler_params=pltpu.CompilerParams(vmem_limit_bytes=VMEM_LIMIT),
+        name="split_blocks",
+    )(qkv_weight[0].transpose(1, 0, 2), out_weight[0], stale_keys[0, 0], stale_values[0, 0])
+    got = [to_core(cut[2 * kind]) for kind in range(5)]
+
+    def blocks_of(layer):
+        pairs = [one for kind in range(5) for one in (cut[2 * kind + 1], got[kind])]
+        flat = pl.pallas_call(
+            functools.partial(choose_kernel, (slots, layer, 5)),
+            out_shape=[b for b in shapes for _ in range(slots)],
+            in_specs=[any_spec()] * 10,
+            out_specs=[any_spec()] * (5 * slots),
+            scratch_shapes=[pltpu.SemaphoreType.DMA((5 * slots,))],
+            compiler_params=pltpu.CompilerParams(vmem_limit_bytes=VMEM_LIMIT),
+            name="choose_blocks",
+        )(*pairs)
+        return [flat[kind * slots : (kind + 1) * slots] for kind in range(5)]
+
+    feats = jnp.pad(embed_time(steps), ((0, 8 - slots), (0, 0)))
+    modulation = pl.pallas_call(
+        functools.partial(mod_kernel, slots),
+        out_shape=jax.ShapeDtypeStruct((slots, 3, feat), jnp.float32),
+        in_specs=[vmem_spec(), vmem_spec()],
+        out_specs=vmem_spec(),
+        compiler_params=pltpu.CompilerParams(vmem_limit_bytes=VMEM_LIMIT),
+        name="modulation",
+    )(feats, mod_weight[0].transpose(1, 0, 2))
+    other_modulation = to_core(modulation)
+    mod_layers = [
+        jnp.where(s == layer, modulation, other_modulation) for layer in range(2)
+    ]
+
+    first_bit, last_bits = group_bits[0], group_bits[1:]
+    lines = {}
+
+    def move(array, bit, depth, *gates):
+        line = lines.setdefault(bit, [])
+        gates = gates + tuple(line[-depth : len(line) - depth + 1] if len(line) >= depth else ())
+        out = to_row(after(array, *gates) if gates else array, bit)
+        line.append(out)
+        return out
+
+    def leave(held, kind, *gates):
+        for d in offsets:
+            held[kind][d ^ first_bit] = move(held[kind][d], first_bit, 2, *gates)
+
+    start = (ends_all,)
+    layers = []
+    for layer in range(2):
+        blocks = blocks_of(layer)
+        gate = start if layer == 0 else (layers[0][1][first_bit],)
+        held = [{0: after(blocks[kind][0], *gate)} for kind in range(5)]
+        for kind in (0, 1, 4, 2, 3):
+            for bit in offsets[1:]:
+                held[kind][bit] = move(blocks[kind][1], bit, 2, *gate)
+        if layer == 0:
+            for kind in range(4):
+                gates = {2: (held[4][offsets[-1]],), 3: tuple(x_chips[1:])}.get(kind, ())
+                leave(held, kind, *gates)
+        layers.append(held)
+    def spread(held, kinds):
+        for kind in kinds:
+            for bit in last_bits:
+                for d in list(held[kind]):
+                    held[kind][d ^ bit] = move(held[kind][d], bit, 4)
+
+    def by_row(held, kinds):
+        return [held[kind][d] for d in range(rows) for kind in kinds]
+
+    def attend(layer, x_pieces, gates):
+        held = layers[layer]
+        plan = (slots, slot_len, cols, len(x_pieces), rows, kr, bw, wc)
+        return pl.pallas_call(
             functools.partial(attend_kernel, plan),
             out_shape=jax.ShapeDtypeStruct((slots * slot_len, bw), jnp.bfloat16),
             in_specs=[pl.BlockSpec(memory_space=pltpu.SMEM), vmem_spec()]
-            + [any_spec()] * (len(x_pieces) + n_w + slots),
+            + [any_spec()] * (len(x_pieces) + 3 * rows + slots),
             out_specs=vmem_spec(),
             scratch_shapes=[
                 pltpu.VMEM((cols, slots * slot_len, wc), jnp.bfloat16),
@@ -302,53 +371,71 @@
                 pltpu.VMEM((3, feat, bw), jnp.bfloat16),
                 pltpu.VMEM((slots, 2, slot_len, bw), jnp.bfloat16),
                 pltpu.SemaphoreType.DMA((len(x_pieces),)),
-                pltpu.SemaphoreType.DMA((n_w,)),
+                pltpu.SemaphoreType.DMA((3 * rows,)),
                 pltpu.SemaphoreType.DMA((slots,)),
             ],
             compiler_params=pltpu.CompilerParams(vmem_limit_bytes=VMEM_LIMIT),
-            cost_estimate=pl.CostEstimate(
-                flops=2 * slots * slot_len * feat * 3 * bw,
-                bytes_accessed=2 * feat * (3 * bw + slots * slot_len),
-                transcendentals=0,
-            ),
             name="attend_layer",
-        )(ends_all, mod_slots[layer], *x_pieces, *qkv_pieces, *stale_slots[layer])
-        plan = (slots, slot_len, cols, n_w, nr, bw, wc)
+        )(
+            after(ends_all, *gates) if gates else ends_all,
+            mod_layers[layer],
+            *x_pieces,
+            *by_row(held, range(3)),
+            *[held[4][d] for d in offsets],
+        )
+
+    def project(layer, attended):
+        plan = (slots, slot_len, cols, rows, nr, bw, wc)
         shape = jax.ShapeDtypeStruct((slots, half, feat), jnp.bfloat16)
-        keep, passed = pl.pallas_call(
+        return pl.pallas_call(
             functools.partial(out_kernel, plan),
             out_shape=(shape, shape),
-            in_specs=[vmem_spec()] + [any_spec()] * n_w,
+            in_specs=[vmem_spec()] + [any_spec()] * rows,
             out_specs=(vmem_spec(), vmem_spec()),
             scratch_shapes=[
-                pltpu.VMEM((feat, bw), jnp.bfloat16),
-                pltpu.SemaphoreType.DMA((n_w,)),
+                pltpu.VMEM((rows, bw, nr), jnp.bfloat16),
+                pltpu.SemaphoreType.DMA((rows,)),
             ],
             compiler_params=pltpu.CompilerParams(vmem_limit_bytes=VMEM_LIMIT),
-            cost_estimate=pl.CostEstimate(
-                flops=2 * slots * slot_len * feat * bw,
-                bytes_accessed=2 * feat * (bw + slots * slot_len),
-                transcendentals=0,
-            ),
             name="project_out",
-        )(attended, *out_pieces)
-        chip_sum = keep.astype(jnp.float32) + to_core(passed).astype(jnp.float32)
-        branch = jnp.zeros((half, wc), jnp.float32)
-        for slot, di in enumerate(offsets):
-            for dc in range(cols):
-                part = chip_sum[slot, :, dc * wc : (dc + 1) * wc]
-                if (di, dc) != (0, 0):
-                    part = send_place(part.astype(jnp.bfloat16), di, dc).astype(jnp.float32)
-                branch = branch + part
-        gate_own = lax.dynamic_slice_in_dim(mod_layers[layer][2], c * wc, wc, 0)
-        updated = x_half.astype(jnp.float32) + gate_own[None, :] * branch
+        )(attended, *by_row(layers[layer], (3,)))
+
+    def chip_parts(keep, passed):
+        chip_sum = keep.astype(jnp.float32) + passed.astype(jnp.float32)
+        return [
+            chip_sum[offsets.index(di), :, dc * wc : (dc + 1) * wc] for di, dc in places
+        ]
+
+    def send_parts(parts):
+        return [send_place(part.astype(jnp.bfloat16), *p) for part, p in zip(parts[1:], places[1:])]
+
+    def finish(layer, x_own, part, arrived):
+        branch = part + sum(one.astype(jnp.float32) for one in arrived)
+        gate_own = lax.dynamic_slice_in_dim(mod_layers[layer][0, 2], c * wc, wc, 0)
+        updated = x_own.astype(jnp.float32) + gate_own[None, :] * branch
         positions = jnp.arange(half)[:, None] + s * half
-        return jnp.where(positions < ends[NP - 1], updated, 0.0).astype(jnp.bfloat16)
-
-    x_half = lax.dynamic_slice_in_dim(hidden_in[0], s * half, half, 0)
-    first = layer_step(0, gather(x_half), x_half)
-    x_pieces = gather(first)
-    second = layer_step(1, x_pieces, first)
+        return jnp.where(positions < patch_ends[0, NP - 1], updated, 0.0).astype(jnp.bfloat16)
+
+    ahead = layers[1]
+    spread(layers[0], range(4))
+    leave(ahead, 0)
+    attended = attend(0, gather(x_chips), (ahead[0][first_bit], ahead[0][offsets[-1]]))
+    leave(ahead, 1)
+    keep, passed = project(0, attended)
+    passed = to_core(after(passed, ahead[1][first_bit], ahead[0][first_bit ^ offsets[-1]]))
+    spread(ahead, (0,))
+    leave(ahead, 2, passed, ahead[4][offsets[-1]])
+    spread(ahead, (1,))
+    parts = chip_parts(keep, passed)
+    arrived = send_parts(parts)
+    leave(ahead, 3, *arrived)
+    spread(ahead, (2, 3))
+    first = finish(0, x_half, parts[0], arrived)
+    x_pieces = gather(gather_chips(first))
+
+    keep, passed = project(1, attend(1, x_pieces, ()))
+    parts = chip_parts(keep, to_core(passed))
+    second = finish(1, first, parts[0], send_parts(parts))
     second_other = to_core(second)
     low = jnp.where(s == 0, first, second_other)
     high = jnp.where(s == 0, x_pieces[1], second)

time: 458 us -> 746 us (1.63)
  Pallas kernels: 41.9 us -> 433 us
  waiting for transfers between devices: 300 us -> 214 us
  local copies, waits for them, and re-layouts: 39.2 us -> 8.82 us
  starting transfers between devices: 51.5 us -> 77.9 us
    pallas_call x4 -> x8, Pallas kernels: 41.9 us -> 433 us  [the longest x2 193 us: blocks_of(): pl.pallas_call(functools.partial(choose_kernel, (slots, layer, 5)), out_s...]
    ppermute x59 -> x88, waiting for transfers between devices: 300 us -> 214 us  [send_to(): return lax.ppermute(array, AXES, pairs)]
    ppermute x59 -> x88, starting transfers between devices: 51.5 us -> 77.9 us  [send_to(): return lax.ppermute(array, AXES, pairs)]
    another operation x7 -> x0, local copies, waits for them, and re-layouts: 8.19 us -> none
  transfers between devices with their start and end apart: 59 -> 88, of which waited for: 28 -> 46; matrix products, arithmetic and copies ran while one was open for 10% -> 1% of each run, Pallas kernels for 7% -> 19%
where the time goes in v2:
time: 746 us; the launch traced here: 745 us
  Pallas kernels  433 us (58%)
  waiting for transfers between devices  214 us (29%)
  starting transfers between devices  77.9 us (10%)
  other arithmetic  10.4 us (1%)
  local copies, waits for them, and re-layouts  8.82 us (1%)
    ppermute x88, waiting for transfers between devices, send_to(): return lax.ppermute(array, AXES, pairs)  214 us
    pallas_call x2, Pallas kernels, blocks_of(): pl.pallas_call(functools.partial(choose_kernel, (slots, layer, 5)), out_s...  193 us
    pallas_call x1, Pallas kernels, shards(): pl.pallas_call(functools.partial(split_kernel, (slots, bw)), out_shape=[b...  192 us
    ppermute x88, starting transfers between devices, send_to(): return lax.ppermute(array, AXES, pairs)  77.9 us
    pallas_call x2, Pallas kernels, attend(): pl.pallas_call(functools.partial(attend_kernel, plan), out_shape=jax.Shap...  31.2 us
  transfers between devices with their start and end apart: 88, of which 46 were waited for; matrix products, arithmetic and copies ran while one was open for 1% of the time, Pallas kernels for 19%

profile of v2, /device:TPU:0, one launch (start us, length us, event | category | flops | bytes accessed | tf_op | source)
XLA Modules:
  0.0 745.1 jit_solution(18011915145843423375)
XLA Ops:
  0.0 191.9 %split_blocks.1 = (bf16[2,384,384]{2,1,0:T(8,128)(2,1)}, bf16[2,384,384]{2,1,0:T(8,128)(2,1)}, bf16[2,384,384]{2,1,0:T(8,128)(2,1)}, bf16[2,384,384]{2,1,0:T(8,1...) custom-call(bf16[3,384,1536]{2,1,0:T(8,128)(2,1)} %bitcast.59, ...), custom_call_target="tpu_custom_call" | custom-call | tf_op jit(solution)/shard_map/split_blocks/pallas_call | solution.py:284
  201.6 96.5 %choose_blocks.3 = (bf16[384,384]{1,0:T(8,128)(2,1)}, bf16[384,384]{1,0:T(8,128)(2,1)}, bf16[384,384]{1,0:T(8,128)(2,1)}, bf16[384,384]{1,0:T(8,128)(2,1)}, bf16...) custom-call(bf16[2,384,384]{2,1,0:T(8,128)(2,1)} %get-tuple-element., ...), custom_call_target="tpu_custom_call" | custom-call | tf_op jit(solution)/shard_map/choose_blocks/pallas_call | solution.py:297
  305.9 8.9 %collective-permute-done.7.refs_20_ = bf16[384,384]{1,0:T(8,128)(2,1)S(1)} collective-permute-done((bf16[384,384]{1,0:T(8,128)(2,1)}, bf16[384,384]{1,0:T(8,128)(2,1)S(1)}, u32[]{:S(2)}, u32[]{:S(2)}) %collective-permute-start.7) | collective-permute-done | bytes 294944 | tf_op jit(solution)/shard_map/ppermute | solution.py:26
  317.7 7.6 %collective-permute-done.17.refs_15_ = bf16[384,384]{1,0:T(8,128)(2,1)S(1)} collective-permute-done((bf16[384,384]{1,0:T(8,128)(2,1)}, bf16[384,384]{1,0:T(8,128)(2,1)S(1)}, u32[]{:S(2)}, u32[]{:S(2)}) %collective-permute-start.17) | collective-permute-done | bytes 294944 | tf_op jit(solution)/shard_map/ppermute | solution.py:26
  327.4 11.1 %collective-permute-done.8.refs_21_ = bf16[384,384]{1,0:T(8,128)(2,1)S(1)} collective-permute-done((bf16[384,384]{1,0:T(8,128)(2,1)}, bf16[384,384]{1,0:T(8,128)(2,1)S(1)}, u32[]{:S(2)}, u32[]{:S(2)}) %collective-permute-start.8) | collective-permute-done | bytes 294944 | tf_op jit(solution)/shard_map/ppermute | solution.py:26
  338.7 4.8 collective-permute-done.33.refs_26_
  349.1 9.2 %collective-permute-done.13.refs_33_ = bf16[2,256,384]{2,1,0:T(8,128)(2,1)S(1)} collective-permute-done((bf16[2,256,384]{2,1,0:T(8,128)(2,1)}, bf16[2,256,384]{2,1,0:T(8,128)(2,1)S(1)}, u32[]{:S(2)}, u32[]{:S(2)}) %collective-permute-start.13) | collective-permute-done | bytes 393248 | tf_op jit(solution)/shard_map/ppermute | solution.py:26
  358.9 4.4 collective-permute-done.34.refs_27_
  366.7 5.0 collective-permute-done.10.refs_4_
  376.1 96.5 %choose_blocks.2 = (bf16[384,384]{1,0:T(8,128)(2,1)}, bf16[384,384]{1,0:T(8,128)(2,1)}, bf16[384,384]{1,0:T(8,128)(2,1)}, bf16[384,384]{1,0:T(8,128)(2,1)}, bf16...) custom-call(bf16[2,384,384]{2,1,0:T(8,128)(2,1)} %get-tuple-element., ...), custom_call_target="tpu_custom_call" | custom-call | tf_op jit(solution)/shard_map/choose_blocks/pallas_call | solution.py:297
  482.3 7.1 collective-permute-done.37.refs_30_
  489.4 5.0 collective-permute-done.40.refs_2_
  504.4 6.3 collective-permute-done.32.refs_25_
  517.1 6.2 collective-permute-done.16.refs_20_
  528.2 6.1 collective-permute-done.39.refs_1_
  535.9 15.6 %attend_layer.2.attended_ref = bf16[512,384]{1,0:T(8,128)(2,1)} custom-call(s32[2,4]{1,0:T(2,128)} %bitcast.63, f32[2,3,3072]{2,1,0:T(4,128)} %get-tuple-element.214.mod_ref, bf16[128,1536]{1,0:T(8,128)(2,1)} %copy-done.7, bf16[128,1536]{1,0:T(8,128)(2,1)} %copy-done.18, bf16[128,1536]{1,0:T(8,128)(2,1)} %copy-done.11, bf16[128,1536]{1,0:T(8,128)(2,1)} %copy-done.19, ...), custom_call_target="tpu_custom_call" | custom-call | tf_op jit(solution)/shard_map/attend_layer/pallas_call | solution.py:362
  553.2 6.4 project_out.2
  565.4 4.8 collective-permute-done.61.refs_15_
  572.5 6.3 collective-permute-done.63.refs_17_
  579.5 5.5 collective-permute-done.68.refs_23_
  604.2 5.3 collective-permute-done.69.refs_24_
  612.6 6.1 collective-permute-done.67.refs_22_
  620.0 8.6 %collective-permute-done.77.refs_2_ = bf16[384,384]{1,0:T(8,128)(2,1)} collective-permute-done((bf16[384,384]{1,0:T(8,128)(2,1)}, bf16[384,384]{1,0:T(8,128)(2,1)}, u32[]{:S(2)}, u32[]{:S(2)}) %collective-permute-start.77) | collective-permute-done | bytes 294944 | tf_op jit(solution)/shard_map/ppermute | solution.py:26
  633.9 11.2 %collective-permute-done.74.refs_30_ = bf16[384,384]{1,0:T(8,128)(2,1)S(1)} collective-permute-done((bf16[384,384]{1,0:T(8,128)(2,1)}, bf16[384,384]{1,0:T(8,128)(2,1)S(1)}, u32[]{:S(2)}, u32[]{:S(2)}) %collective-permute-start.74) | collective-permute-done | bytes 294944 | tf_op jit(solution)/shard_map/ppermute | solution.py:26
  656.0 8.1 %collective-permute-done.54.refs_4_ = bf16[128,1536]{1,0:T(8,128)(2,1)S(1)} collective-permute-done((bf16[128,1536]{1,0:T(8,128)(2,1)S(1)}, bf16[128,1536]{1,0:T(8,128)(2,1)S(1)}, u32[]{:S(2)}, u32[]{:S(2)}) %collective-permute-start.54) | collective-permute-done | bytes 393248 | tf_op jit(solution)/shard_map/ppermute | solution.py:26
  664.9 6.1 collective-permute-done.56.refs_6_
  671.0 9.4 %collective-permute-done.81.refs_6_ = bf16[384,384]{1,0:T(8,128)(2,1)S(1)} collective-permute-done((bf16[384,384]{1,0:T(8,128)(2,1)}, bf16[384,384]{1,0:T(8,128)(2,1)S(1)}, u32[]{:S(2)}, u32[]{:S(2)}) %collective-permute-start.81) | collective-permute-done | bytes 294944 | tf_op jit(solution)/shard_map/ppermute | solution.py:26
  685.3 15.6 %attend_layer.3.attended_ref = bf16[512,384]{1,0:T(8,128)(2,1)} custom-call(s32[2,4]{1,0:T(2,128)} %bitcast.64, f32[2,3,3072]{2,1,0:T(4,128)} %get-tuple-element.213.mod_ref, bf16[128,1536]{1,0:T(8,128)(2,1)} %copy-done, bf16[128,1536]{1,0:T(8,128)(2,1)} %copy-done.8, bf16[128,1536]{1,0:T(8,128)(2,1)} %copy-done.16, bf16[128,1536]{1,0:T(8,128)(2,1)} %copy-done.23, ...), custom_call_target="tpu_custom_call" | custom-call | tf_op jit(solution)/shard_map/attend_layer/pallas_call | solution.py:362
  703.2 5.2 collective-permute-done.82.refs_7_
  709.1 6.4 project_out.3
  725.8 8.6 %collective-permute-done.86 = bf16[128,1536]{1,0:T(8,128)(2,1)S(1)} collective-permute-done((bf16[128,1536]{1,0:T(8,128)(2,1)S(1)}, bf16[128,1536]{1,0:T(8,128)(2,1)S(1)}, u32[]{:S(2)}, u32[]{:S(2)}) %collective-permute-start.86) | collective-permute-done | bytes 393248 | tf_op jit(solution)/shard_map/ppermute | solution.py:26
  734.4 5.9 collective-permute-done.85
  (351 shorter events, 141.9 us)
Async XLA Ops:
  301.8 23.5 %collective-permute-start.9 = (bf16[128,1536]{1,0:T(8,128)(2,1)S(1)}, bf16[128,1536]{1,0:T(8,128)(2,1)S(1)}, u32[]{:S(2)}, u32[]{:S(2)}) collective-permute-start(bf16[128,1536]{1,0:T(8,128)(2,1)S(1)} %dynamic-slice_bitcast_fusion.refs_0_), channel_id=1, source_target_pairs={{0,1},{1,0},{2,3},{3,2},{4,5},{5,4},{6,7},{7,6},{8,9},{9,8},{10,11... | collective-permute-start | bytes 1179656 | tf_op jit(solution)/shard_map/ppermute | solution.py:26
  303.3 22.0 %collective-permute-start.17 = (bf16[384,384]{1,0:T(8,128)(2,1)}, bf16[384,384]{1,0:T(8,128)(2,1)S(1)}, u32[]{:S(2)}, u32[]{:S(2)}) collective-permute-start(bf16[384,384]{1,0:T(8,128)(2,1)} %get-tuple-element.134), channel_id=1, source_target_pairs={{0,4},{1,5},{2,6},{3,7},{4,0},{5,1},{6,2},{7,3},{8,12},{9,13},{10,... | collective-permute-start | bytes 884744 | tf_op jit(solution)/shard_map/ppermute | solution.py:26
  304.3 22.6 %collective-permute-start.24 = (bf16[384,384]{1,0:T(8,128)(2,1)}, bf16[384,384]{1,0:T(8,128)(2,1)S(1)}, u32[]{:S(2)}, u32[]{:S(2)}) collective-permute-start(bf16[384,384]{1,0:T(8,128)(2,1)} %get-tuple-element.117.refs_8_), channel_id=1, source_target_pairs={{0,2},{1,3},{2,0},{3,1},{4,6},{5,7},{6,4},{7,5},{8,10},{9,11},{10,... | collective-permute-start | bytes 884744 | tf_op jit(solution)/shard_map/ppermute | solution.py:26
  314.8 23.7 %collective-permute-start.8 = (bf16[384,384]{1,0:T(8,128)(2,1)}, bf16[384,384]{1,0:T(8,128)(2,1)S(1)}, u32[]{:S(2)}, u32[]{:S(2)}) collective-permute-start(bf16[384,384]{1,0:T(8,128)(2,1)} %get-tuple-element.138.refs_9_), channel_id=1, source_target_pairs={{0,8},{1,9},{2,10},{3,11},{4,12},{5,13},{6,14},{7,15},{8,0},{9,1},... | collective-permute-start | bytes 884744 | tf_op jit(solution)/shard_map/ppermute | solution.py:26
  316.7 26.9 %collective-permute-start.33 = (bf16[384,384]{1,0:T(8,128)(2,1)S(1)}, bf16[384,384]{1,0:T(8,128)(2,1)S(1)}, u32[]{:S(2)}, u32[]{:S(2)}) collective-permute-start(bf16[384,384]{1,0:T(8,128)(2,1)S(1)} %collective-permute-done.12.refs_14_), channel_id=1, source_target_pairs={{0,8},{1,9},{2,10},{3,11},{4,12},{5,13},{6,14},{7,15},{8,0},{9,1},... | collective-permute-start | bytes 884744 | tf_op jit(solution)/shard_map/ppermute | solution.py:26
  325.3 21.6 %collective-permute-start.27 = (bf16[384,384]{1,0:T(8,128)(2,1)S(1)}, bf16[384,384]{1,0:T(8,128)(2,1)S(1)}, u32[]{:S(2)}, u32[]{:S(2)}) collective-permute-start(bf16[384,384]{1,0:T(8,128)(2,1)S(1)} %collective-permute-done.12.refs_14_), channel_id=1, source_target_pairs={{0,2},{1,3},{2,0},{3,1},{4,6},{5,7},{6,4},{7,5},{8,10},{9,11},{10,... | collective-permute-start | bytes 884744 | tf_op jit(solution)/shard_map/ppermute | solution.py:26
  326.9 21.5 %collective-permute-start.30 = (bf16[384,384]{1,0:T(8,128)(2,1)S(1)}, bf16[384,384]{1,0:T(8,128)(2,1)S(1)}, u32[]{:S(2)}, u32[]{:S(2)}) collective-permute-start(bf16[384,384]{1,0:T(8,128)(2,1)S(1)} %collective-permute-done.7.refs_20_), channel_id=1, source_target_pairs={{0,2},{1,3},{2,0},{3,1},{4,6},{5,7},{6,4},{7,5},{8,10},{9,11},{10,... | collective-permute-start | bytes 884744 | tf_op jit(solution)/shard_map/ppermute | solution.py:26
  343.6 28.1 %collective-permute-start.10 = (bf16[128,1536]{1,0:T(8,128)(2,1)S(1)}, bf16[128,1536]{1,0:T(8,128)(2,1)S(1)}, u32[]{:S(2)}, u32[]{:S(2)}) collective-permute-start(bf16[128,1536]{1,0:T(8,128)(2,1)S(1)} %dynamic-slice_bitcast_fusion.refs_0_), channel_id=1, source_target_pairs={{0,4},{1,5},{2,6},{3,7},{4,0},{5,1},{6,2},{7,3},{8,12},{9,13},{10,... | collective-permute-start | bytes 1179656 | tf_op jit(solution)/shard_map/ppermute | solution.py:26
  346.9 26.3 %collective-permute-start.25 = (bf16[384,384]{1,0:T(8,128)(2,1)}, bf16[384,384]{1,0:T(8,128)(2,1)S(1)}, u32[]{:S(2)}, u32[]{:S(2)}) collective-permute-start(bf16[384,384]{1,0:T(8,128)(2,1)} %get-tuple-element.138.refs_9_), channel_id=1, source_target_pairs={{0,2},{1,3},{2,0},{3,1},{4,6},{5,7},{6,4},{7,5},{8,10},{9,11},{10,... | collective-permute-start | bytes 884744 | tf_op jit(solution)/shard_map/ppermute | solution.py:26
  348.4 25.2 %collective-permute-start.36 = (bf16[384,384]{1,0:T(8,128)(2,1)S(1)}, bf16[384,384]{1,0:T(8,128)(2,1)S(1)}, u32[]{:S(2)}, u32[]{:S(2)}) collective-permute-start(bf16[384,384]{1,0:T(8,128)(2,1)S(1)} %collective-permute-done.33.refs_26_), channel_id=1, source_target_pairs={{0,2},{1,3},{2,0},{3,1},{4,6},{5,7},{6,4},{7,5},{8,10},{9,11},{10,... | collective-permute-start | bytes 884744 | tf_op jit(solution)/shard_map/ppermute | solution.py:26
  358.3 114.5 %collective-permute-start.11 = (bf16[128,1536]{1,0:T(8,128)(2,1)S(1)}, bf16[128,1536]{1,0:T(8,128)(2,1)S(1)}, u32[]{:S(2)}, u32[]{:S(2)}) collective-permute-start(bf16[128,1536]{1,0:T(8,128)(2,1)S(1)} %dynamic-slice_bitcast_fusion.refs_0_), channel_id=1, source_target_pairs={{0,5},{1,4},{2,7},{3,6},{4,1},{5,0},{6,3},{7,2},{8,13},{9,12},{10,... | collective-permute-start | bytes 1179656 | tf_op jit(solution)/shard_map/ppermute | solution.py:26
  363.3 112.1 %collective-permute-start.14 = (bf16[384,384]{1,0:T(8,128)(2,1)}, bf16[384,384]{1,0:T(8,128)(2,1)S(1)}, u32[]{:S(2)}, u32[]{:S(2)}) collective-permute-start(bf16[384,384]{1,0:T(8,128)(2,1)} %get-tuple-element.139.refs_10_), channel_id=1, source_target_pairs={{0,8},{1,9},{2,10},{3,11},{4,12},{5,13},{6,14},{7,15},{8,0},{9,1},... | collective-permute-start | bytes 884744 | tf_op jit(solution)/shard_map/ppermute | solution.py:26
  371.6 105.3 %collective-permute-start.28 = (bf16[384,384]{1,0:T(8,128)(2,1)S(1)}, bf16[384,384]{1,0:T(8,128)(2,1)S(1)}, u32[]{:S(2)}, u32[]{:S(2)}) collective-permute-start(bf16[384,384]{1,0:T(8,128)(2,1)S(1)} %collective-permute-done.17.refs_15_), channel_id=1, source_target_pairs={{0,2},{1,3},{2,0},{3,1},{4,6},{5,7},{6,4},{7,5},{8,10},{9,11},{10,... | collective-permute-start | bytes 884744 | tf_op jit(solution)/shard_map/ppermute | solution.py:26
  373.2 103.9 %collective-permute-start.31 = (bf16[384,384]{1,0:T(8,128)(2,1)S(1)}, bf16[384,384]{1,0:T(8,128)(2,1)S(1)}, u32[]{:S(2)}, u32[]{:S(2)}) collective-permute-start(bf16[384,384]{1,0:T(8,128)(2,1)S(1)} %collective-permute-done.8.refs_21_), channel_id=1, source_target_pairs={{0,2},{1,3},{2,0},{3,1},{4,6},{5,7},{6,4},{7,5},{8,10},{9,11},{10,... | collective-permute-start | bytes 884744 | tf_op jit(solution)/shard_map/ppermute | solution.py:26
  373.7 103.9 %collective-permute-start.35 = (bf16[384,384]{1,0:T(8,128)(2,1)S(1)}, bf16[384,384]{1,0:T(8,128)(2,1)S(1)}, u32[]{:S(2)}, u32[]{:S(2)}) collective-permute-start(bf16[384,384]{1,0:T(8,128)(2,1)S(1)} %collective-permute-done.18.refs_16_), channel_id=1, source_target_pairs={{0,8},{1,9},{2,10},{3,11},{4,12},{5,13},{6,14},{7,15},{8,0},{9,1},... | collective-permute-start | bytes 884744 | tf_op jit(solution)/shard_map/ppermute | solution.py:26
  472.8 23.7 %collective-permute-start.19 = (bf16[384,384]{1,0:T(8,128)(2,1)}, bf16[384,384]{1,0:T(8,128)(2,1)}, u32[]{:S(2)}, u32[]{:S(2)}) collective-permute-start(bf16[384,384]{1,0:T(8,128)(2,1)} %get-tuple-element.136), channel_id=1, source_target_pairs={{0,4},{1,5},{2,6},{3,7},{4,0},{5,1},{6,2},{7,3},{8,12},{9,13},{10,... | collective-permute-start | bytes 884744 | tf_op jit(solution)/shard_map/ppermute | solution.py:26
  475.3 22.7 %collective-permute-start.26 = (bf16[384,384]{1,0:T(8,128)(2,1)S(1)}, bf16[384,384]{1,0:T(8,128)(2,1)S(1)}, u32[]{:S(2)}, u32[]{:S(2)}) collective-permute-start(bf16[384,384]{1,0:T(8,128)(2,1)S(1)} %copy-done.32), channel_id=1, source_target_pairs={{0,2},{1,3},{2,0},{3,1},{4,6},{5,7},{6,4},{7,5},{8,10},{9,11},{10,... | collective-permute-start | bytes 884744 | tf_op jit(solution)/shard_map/ppermute | solution.py:26
  498.0 25.3 %collective-permute-start.16 = (bf16[384,384]{1,0:T(8,128)(2,1)S(1)}, bf16[384,384]{1,0:T(8,128)(2,1)S(1)}, u32[]{:S(2)}, u32[]{:S(2)}) collective-permute-start(bf16[384,384]{1,0:T(8,128)(2,1)S(1)} %copy-done.26), channel_id=1, source_target_pairs={{0,8},{1,9},{2,10},{3,11},{4,12},{5,13},{6,14},{7,15},{8,0},{9,1},... | collective-permute-start | bytes 884744 | tf_op jit(solution)/shard_map/ppermute | solution.py:26
  524.6 27.0 %collective-permute-start.41 = (bf16[384,384]{1,0:T(8,128)(2,1)}, bf16[384,384]{1,0:T(8,128)(2,1)S(1)}, u32[]{:S(2)}, u32[]{:S(2)}) collective-permute-start(bf16[384,384]{1,0:T(8,128)(2,1)} %copy-done.70), channel_id=1, source_target_pairs={{0,2},{1,3},{2,0},{3,1},{4,6},{5,7},{6,4},{7,5},{8,10},{9,11},{10,... | collective-permute-start | bytes 884744 | tf_op jit(solution)/shard_map/ppermute | solution.py:26
  526.1 25.5 %collective-permute-start.42 = (bf16[384,384]{1,0:T(8,128)(2,1)}, bf16[384,384]{1,0:T(8,128)(2,1)S(1)}, u32[]{:S(2)}, u32[]{:S(2)}) collective-permute-start(bf16[384,384]{1,0:T(8,128)(2,1)} %copy-done.71), channel_id=1, source_target_pairs={{0,2},{1,3},{2,0},{3,1},{4,6},{5,7},{6,4},{7,5},{8,10},{9,11},{10,... | collective-permute-start | bytes 884744 | tf_op jit(solution)/shard_map/ppermute | solution.py:26
  526.6 25.5 %collective-permute-start.44 = (bf16[384,384]{1,0:T(8,128)(2,1)}, bf16[384,384]{1,0:T(8,128)(2,1)S(1)}, u32[]{:S(2)}, u32[]{:S(2)}) collective-permute-start(bf16[384,384]{1,0:T(8,128)(2,1)} %copy-done.72), channel_id=1, source_target_pairs={{0,2},{1,3},{2,0},{3,1},{4,6},{5,7},{6,4},{7,5},{8,10},{9,11},{10,... | collective-permute-start | bytes 884744 | tf_op jit(solution)/shard_map/ppermute | solution.py:26
  528.2 31.4 %collective-permute-start.46 = (bf16[384,384]{1,0:T(8,128)(2,1)}, bf16[384,384]{1,0:T(8,128)(2,1)S(1)}, u32[]{:S(2)}, u32[]{:S(2)}) collective-permute-start(bf16[384,384]{1,0:T(8,128)(2,1)} %collective-permute-done.19.refs_14_), channel_id=1, source_target_pairs={{0,8},{1,9},{2,10},{3,11},{4,12},{5,13},{6,14},{7,15},{8,0},{9,1},... | collective-permute-start | bytes 884744 | tf_op jit(solution)/shard_map/ppermute | solution.py:26
  534.3 25.3 %collective-permute-start.45 = (bf16[384,384]{1,0:T(8,128)(2,1)}, bf16[384,384]{1,0:T(8,128)(2,1)S(1)}, u32[]{:S(2)}, u32[]{:S(2)}) collective-permute-start(bf16[384,384]{1,0:T(8,128)(2,1)} %get-tuple-element.167.refs_9_), channel_id=1, source_target_pairs={{0,8},{1,9},{2,10},{3,11},{4,12},{5,13},{6,14},{7,15},{8,0},{9,1},... | collective-permute-start | bytes 884744 | tf_op jit(solution)/shard_map/ppermute | solution.py:26
  559.6 26.2 %collective-permute-start.47 = (bf16[2,128,3072]{2,1,0:T(8,128)(2,1)}, bf16[2,128,3072]{2,1,0:T(8,128)(2,1)S(1)}, u32[]{:S(2)}, u32[]{:S(2)}) collective-permute-start(bf16[2,128,3072]{2,1,0:T(8,128)(2,1)} %get-tuple-element.163), channel_id=1, source_target_pairs={{0,16},{1,17},{2,18},{3,19},{4,20},{5,21},{6,22},{7,23},{8,24},{9,... | collective-permute-start | bytes 4718600 | tf_op jit(solution)/shard_map/ppermute | solution.py:26
  591.4 38.8 %collective-permute-start.50 = (bf16[128,1536]{1,0:T(8,128)(2,1)}, bf16[128,1536]{1,0:T(8,128)(2,1)}, u32[]{:S(2)}, u32[]{:S(2)}) collective-permute-start(bf16[128,1536]{1,0:T(8,128)(2,1)} %get-tuple-element.211), channel_id=1, source_target_pairs={{0,5},{1,4},{2,7},{3,6},{4,1},{5,0},{6,3},{7,2},{8,13},{9,12},{10,... | collective-permute-start | bytes 1179656 | tf_op jit(solution)/shard_map/ppermute | solution.py:26
  597.7 33.0 %collective-permute-start.49 = (bf16[128,1536]{1,0:T(8,128)(2,1)}, bf16[128,1536]{1,0:T(8,128)(2,1)}, u32[]{:S(2)}, u32[]{:S(2)}) collective-permute-start(bf16[128,1536]{1,0:T(8,128)(2,1)} %get-tuple-element.212), channel_id=1, source_target_pairs={{0,4},{1,5},{2,6},{3,7},{4,0},{5,1},{6,2},{7,3},{8,12},{9,13},{10,... | collective-permute-start | bytes 1179656 | tf_op jit(solution)/shard_map/ppermute | solution.py:26
  600.3 30.3 %collective-permute-start.48 = (bf16[128,1536]{1,0:T(8,128)(2,1)}, bf16[128,1536]{1,0:T(8,128)(2,1)}, u32[]{:S(2)}, u32[]{:S(2)}) collective-permute-start(bf16[128,1536]{1,0:T(8,128)(2,1)} %get-tuple-element.210), channel_id=1, source_target_pairs={{0,1},{1,0},{2,3},{3,2},{4,5},{5,4},{6,7},{7,6},{8,9},{9,8},{10,11... | collective-permute-start | bytes 1179656 | tf_op jit(solution)/shard_map/ppermute | solution.py:26
  618.7 26.9 %collective-permute-start.60 = (bf16[384,384]{1,0:T(8,128)(2,1)}, bf16[384,384]{1,0:T(8,128)(2,1)S(1)}, u32[]{:S(2)}, u32[]{:S(2)}) collective-permute-start(bf16[384,384]{1,0:T(8,128)(2,1)} %get-tuple-element.178.refs_10_), channel_id=1, source_target_pairs={{0,2},{1,3},{2,0},{3,1},{4,6},{5,7},{6,4},{7,5},{8,10},{9,11},{10,... | collective-permute-start | bytes 884744 | tf_op jit(solution)/shard_map/ppermute | solution.py:26
  655.4 26.1 %collective-permute-start.51 = (bf16[128,1536]{1,0:T(8,128)(2,1)S(1)}, bf16[128,1536]{1,0:T(8,128)(2,1)S(1)}, u32[]{:S(2)}, u32[]{:S(2)}) collective-permute-start(bf16[128,1536]{1,0:T(8,128)(2,1)S(1)} %fusion.9.refs_0_), channel_id=1, source_target_pairs={{0,16},{1,17},{2,18},{3,19},{4,20},{5,21},{6,22},{7,23},{8,24},{9,... | collective-permute-start | bytes 1179656 | tf_op jit(solution)/shard_map/ppermute | solution.py:26
  655.5 27.1 %collective-permute-start.53 = (bf16[128,1536]{1,0:T(8,128)(2,1)S(1)}, bf16[128,1536]{1,0:T(8,128)(2,1)S(1)}, u32[]{:S(2)}, u32[]{:S(2)}) collective-permute-start(bf16[128,1536]{1,0:T(8,128)(2,1)S(1)} %collective-permute-done.52.refs_2_), channel_id=1, source_target_pairs={{0,16},{1,17},{2,18},{3,19},{4,20},{5,21},{6,22},{7,23},{8,24},{9,... | collective-permute-start | bytes 1179656 | tf_op jit(solution)/shard_map/ppermute | solution.py:26
  682.5 20.7 %collective-permute-start.80 = (bf16[384,384]{1,0:T(8,128)(2,1)S(1)}, bf16[384,384]{1,0:T(8,128)(2,1)S(1)}, u32[]{:S(2)}, u32[]{:S(2)}) collective-permute-start(bf16[384,384]{1,0:T(8,128)(2,1)S(1)} %collective-permute-done.79.refs_4_), channel_id=1, source_target_pairs={{0,2},{1,3},{2,0},{3,1},{4,6},{5,7},{6,4},{7,5},{8,10},{9,11},{10,... | collective-permute-start | bytes 884744 | tf_op jit(solution)/shard_map/ppermute | solution.py:26
  683.6 24.8 %collective-permute-start.82 = (bf16[384,384]{1,0:T(8,128)(2,1)S(1)}, bf16[384,384]{1,0:T(8,128)(2,1)S(1)}, u32[]{:S(2)}, u32[]{:S(2)}) collective-permute-start(bf16[384,384]{1,0:T(8,128)(2,1)S(1)} %collective-permute-done.81.refs_6_), channel_id=1, source_target_pairs={{0,2},{1,3},{2,0},{3,1},{4,6},{5,7},{6,4},{7,5},{8,10},{9,11},{10,... | collective-permute-start | bytes 884744 | tf_op jit(solution)/shard_map/ppermute | solution.py:26
  (144 other events, 4492.0 us)
